TPU v7x, 256 devices: a whole 4x4x8 slice. The times are simulated.
256 devices in a mesh: leaf: 64 (over y, z, core), rhs: 4 (over x).
Axes of the slice: x: 4, y: 4, z: 8, core: 2. Of those that a mesh axis runs over, the one named last changes fastest.
Arguments:
- leaf_right: float32 [2048, 256, 128], P('leaf', 'rhs'), may hold values from -6 to 6
- upper_right: float32 [128, 256, 128], P('leaf', 'rhs'), may hold values from -6 to 6
- leaf_inverse: bfloat16 [2048, 128, 128], P(('leaf', 'rhs')), as said below
- upper_inverse: bfloat16 [128, 128, 128], P('leaf'), as said below
- update_blocks: bfloat16 [16384, 128, 128], P('leaf'), may hold values from -0.046875 to 0.046875
- block_target: int32 [16384, 1], P('leaf'), may hold values from 0 to 127; in each aligned block of 256 rows (0 to 255, 256 to 511, ...) at most 4 rows name the same one
- upper_place: int32 [128], replicated, may hold values from 0 to 127, each once
Outputs:
- leaf_solution: float32 [2048, 256, 128], P('leaf', 'rhs')
- upper_solution: float32 [128, 256, 128], P('leaf', 'rhs')
Inputs may be any that keep to these rules, and one draw needn't show every extreme that they name: `leaf_inverse`: lower triangular blocks, diagonal entries between 0.6 and 1.4. `upper_inverse`: lower triangular blocks, diagonal entries between 0.6 and 1.4. `block_target`: among the 256 blocks of one device no upper supernode is named more than 4 times, a bound that some block reaches. `upper_place`: each row of the upper arrays holds exactly one upper supernode.
All inputs are finite; a program needn't handle non-finite values.
Results may differ from a plain program's by a relative error of at most 0.0049.
Values may be sent and summed in bfloat16 or wider, within the bound.
A program may use at most 64 MiB of HBM per device.

v0:
```python
import jax
import jax.numpy as jnp
from jax import lax
from jax.sharding import PartitionSpec as P


def on_device(
    leaf_right, upper_right, leaf_inverse, upper_inverse, update_blocks, block_target, upper_place
):
    inverse_mine = lax.all_gather(leaf_inverse, "rhs", axis=0, tiled=True)
    leaf_rounded = leaf_right.astype(jnp.bfloat16)
    leaf_forward = jnp.einsum(
        "ncw,nvw->ncv", leaf_rounded, inverse_mine, preferred_element_type=jnp.float32
    )
    leaf_half = leaf_forward.astype(jnp.bfloat16)
    leaf_count, columns, width = leaf_forward.shape
    block_count = update_blocks.shape[0]
    per_leaf = block_count // leaf_count
    grouped = update_blocks.reshape(leaf_count, per_leaf, width, width)
    updates = jnp.einsum("ncw,nbvw->nbcv", leaf_half, grouped, preferred_element_type=jnp.float32)
    updates = updates.reshape(block_count, columns, width)
    upper_total = upper_place.shape[0]
    table = jnp.arange(upper_total, dtype=jnp.int32)
    position = jnp.sum(jnp.where(block_target == table[None, :], upper_place[None, :], 0), axis=1)
    upper_rows = upper_right.shape[0]
    local_index = position
    inside = (local_index >= 0) & (local_index < upper_rows * lax.axis_size("leaf"))
    local_index = jnp.where(inside, local_index, upper_rows * lax.axis_size("leaf"))
    upper_sums = lax.psum_scatter(
        jax.ops.segment_sum(updates, local_index, num_segments=upper_rows * lax.axis_size("leaf")),
        "leaf",
        scatter_dimension=0,
        tiled=True,
    )
    upper_rounded = (upper_right - upper_sums).astype(jnp.bfloat16)
    upper_half = jnp.einsum(
        "pcw,pvw->pcv", upper_rounded, upper_inverse, preferred_element_type=jnp.float32
    ).astype(jnp.bfloat16)
    upper_solution = jnp.einsum(
        "pcw,pwv->pcv", upper_half, upper_inverse, preferred_element_type=jnp.float32
    )
    upper_sent = upper_solution.astype(jnp.bfloat16)
    solved_table = lax.all_gather(upper_sent, "leaf", axis=0, tiled=True)
    chosen = jnp.take(solved_table, position, axis=0)
    corrections = jnp.einsum(
        "kcv,kvw->kcw", chosen, update_blocks, preferred_element_type=jnp.float32
    )
    corrections = corrections.reshape(leaf_count, per_leaf, columns, width).sum(axis=1)
    leaf_back = (leaf_forward - corrections).astype(jnp.bfloat16)
    leaf_solution = jnp.einsum(
        "ncw,nwv->ncv", leaf_back, inverse_mine, preferred_element_type=jnp.float32
    )
    return (leaf_solution, upper_solution)


def solution(mesh):
    return jax.shard_map(
        on_device,
        mesh=mesh,
        in_specs=(
            P("leaf", "rhs", None),
            P("leaf", "rhs", None),
            P(("leaf", "rhs"), None, None),
            P("leaf", None, None),
            P("leaf", None, None),
            P("leaf", None),
            P(),
        ),
        out_specs=(P("leaf", "rhs", None), P("leaf", "rhs", None)),
        check_vma=False,
    )
```

profile of v0, /device:TPU:1, one launch (start us, length us, event | category | flops | bytes accessed | tf_op | source)
XLA Modules:
  0.0 338.5 jit_solution(17346281940933567968)
XLA Ops:
  7.2 0.0 copy-start
  7.2 0.0 all-gather.3.cloned.1.call-start
  7.2 0.7 all-gather.3.cloned.1.call-update
  7.9 0.0 reduce-scatter.2.cloned.1.call-start
  8.0 0.9 select_reduce_fusion
  8.8 30.4 %all-gather.3.cloned.1.call-done = bf16[32,128,128]{2,1,0:T(8,128)(2,1)} async-done(((bf16[8,128,128]{2,1,0:T(8,128)(2,1)}), bf16[32,128,128]{2,1,0:T(8,128)(2,1)}) %all-gather.3.cloned.1.call-update) | async-done | bytes 1048592 | tf_op jit(solution)/shard_map/all_gather | solution.py:10
  39.2 2.3 fusion.11
  41.6 9.6 %fusion.8 = f32[32,64,8,128]{3,1,2,0:T(8,128)} fusion(bf16[32,8,128,128]{3,2,1,0:T(8,128)(2,1)} %bitcast.22, f32[32,64,128]{2,1,0:T(8,128)S(1)} %fusion.11), kind=kOutput, calls=%fused_computation.11 | convolution fusion | flops 537133056 | bytes 17825792 | tf_op jit(solution)/shard_map/ncw,nbvw->nbcv/dot_general | solution.py:20
  51.2 2.5 broadcast_in_dim.33
  53.7 39.9 %scatter_fusion = f32[128,64,128]{2,1,0:T(8,128)} fusion(f32[128,64,128]{2,1,0:T(8,128)} %broadcast_in_dim.33, s32[256]{0:T(256)S(1)} %bitcast.23, f32[256,64,128]{2,1,0:T(8,128)} %bitcast.21), kind=kCustom, calls=%fused_computation.1 | custom fusion | flops 2097152 | bytes 25166848 | tf_op jit(solution)/shard_map/scatter-add | solution.py:30
  93.6 0.0 copy-start.2
  93.6 0.0 reduce-scatter.2.cloned.1.call-update
  93.6 0.0 all-gather.5.cloned.1.call-start
  93.6 140.2 %reduce-scatter.2.cloned.1.call-done = f32[2,64,128]{2,1,0:T(8,128)} async-done(((f32[128,64,128]{2,1,0:T(8,128)}), f32[2,64,128]{2,1,0:T(8,128)}) %reduce-scatter.2.cloned.1.call-update) | async-done | bytes 65552 | tf_op jit(solution)/shard_map/reduce_scatter | solution.py:29
  233.9 0.0 copy-done
  233.9 0.0 copy-done.2
  233.9 1.7 fusion.14
  235.6 0.0 all-gather.5.cloned.1.call-update
  235.7 83.0 %all-gather.5.cloned.1.call-done = bf16[128,64,128]{2,1,0:T(8,128)(2,1)} async-done(((bf16[2,64,128]{2,1,0:T(8,128)(2,1)}), bf16[128,64,128]{2,1,0:T(8,128)(2,1)}) %all-gather.5.cloned.1.call-update) | async-done | bytes 2097168 | tf_op jit(solution)/shard_map/all_gather | solution.py:43
  318.7 4.6 %gather_fusion = bf16[256,64,128]{2,1,0:T(8,128)(2,1)} fusion(bf16[128,64,128]{2,1,0:T(8,128)(2,1)} %all-gather.5.cloned.1.call-done, s32[1024]{0:T(1024)S(1)} %pad_clamp_fusion), kind=kCustom, calls=%fused_computation | custom fusion | bytes 8389632 | tf_op jit(solution)/shard_map/jit(_take)/gather | solution.py:44
  323.3 0.0 copy-start.1
  323.3 7.2 %bitcast_reduce_fusion = f32[32,64,128]{2,1,0:T(8,128)S(1)} fusion(bf16[256,128,128]{2,1,0:T(8,128)(2,1)} %param.11, bf16[256,64,128]{2,1,0:T(8,128)(2,1)} %gather_fusion, pred[256]{0:T(512)(128)(4,1)S(1)} %compare_and_fusion), kind=kOutput, calls=%fused_computation.2 | convolution fusion | flops 540803072 | bytes 13631744 | tf_op jit(solution)/shard_map/kcv,kvw->kcw/dot_general | solution.py:45
  330.5 0.0 copy-done.1
  330.5 1.4 fusion.7
  (3 shorter events, 0.0 us)
Async XLA Ops:
  7.2 226.7 %copy-start = (bf16[2,128,128]{2,1,0:T(8,128)(2,1)S(1)}, bf16[2,128,128]{2,1,0:T(8,128)(2,1)}, u32[]{:S(2)}) copy-start(bf16[2,128,128]{2,1,0:T(8,128)(2,1)} %param.10) | copy-start | bytes 196612
  7.2 32.1 %all-gather.3.cloned.1.call-start = ((), (), s32[]{:S(2)}) async-start(), calls=%async_computation.1 | async-start | bytes 1310720 | tf_op jit(solution)/shard_map/all_gather | solution.py:10
  7.9 226.0 %reduce-scatter.2.cloned.1.call-start = ((), (), s32[]{:S(2)}) async-start(), calls=%async_computation.2 | async-start | bytes 4259840 | tf_op jit(solution)/shard_map/reduce_scatter | solution.py:29
  93.6 140.3 %copy-start.2 = (f32[2,64,128]{2,1,0:T(8,128)S(1)}, f32[2,64,128]{2,1,0:T(8,128)}, u32[]{:S(2)}) copy-start(f32[2,64,128]{2,1,0:T(8,128)} %param.8) | copy-start | bytes 196612
  93.6 225.1 %all-gather.5.cloned.1.call-start = ((), (), s32[]{:S(2)}) async-start(), calls=%async_computation.3 | async-start | bytes 2129920 | tf_op jit(solution)/shard_map/all_gather | solution.py:43
  323.3 7.2 %copy-start.1 = (bf16[32,128,128]{2,1,0:T(8,128)(2,1)S(1)}, bf16[32,128,128]{2,1,0:T(8,128)(2,1)}, u32[]{:S(2)}) copy-start(bf16[32,128,128]{2,1,0:T(8,128)(2,1)} %all-gather.3.cloned.1.call-done) | copy-start | bytes 3145732
Sparse Core Ops, SparseCore 0:
  9.8 29.3 all-gather.2
  93.7 140.1 reduce-scatter.1
  237.6 81.0 all-gather.4
where the time goes:
time: 339 us; the launch traced here: 338 us
  waiting for transfers between devices  254 us (75%)
  other arithmetic  40.7 us (12%)
  matrix products  22.3 us (7%)
  between operations  13.8 us (4%)
  local copies, waits for them, and re-layouts  7.11 us (2%)
    reduce_scatter x1, waiting for transfers between devices, on_device(): lax.psum_scatter(jax.ops.segment_sum(updates, local_index, num_segments=u...  140 us
    all_gather x1, waiting for transfers between devices, on_device(): solved_table = lax.all_gather(upper_sent, 'leaf', axis=0, tiled=True)  83 us
    scatter-add x1, other arithmetic, on_device(): jax.ops.segment_sum(updates, local_index, num_segments=upper_rows * lax.a...  39.9 us
    all_gather x1, waiting for transfers between devices, on_device(): inverse_mine = lax.all_gather(leaf_inverse, 'rhs', axis=0, tiled=True)  30.4 us
    dot_general x1, matrix products, on_device(): jnp.einsum('ncw,nbvw->nbcv', leaf_half, grouped, preferred_element_type=j...  9.63 us
    dot_general x1, matrix products, on_device(): jnp.einsum('kcv,kvw->kcw', chosen, update_blocks, preferred_element_type=...  7.16 us
  transfers between devices with their start and end apart: 3, of which 3 were waited for; matrix products, arithmetic and copies ran while one was open for 0% of the time, Pallas kernels for 0%

commit v1 on v0

v1 whole, which is shorter than its diff:
```python
import functools

import jax
import jax.numpy as jnp
from jax import lax
from jax.experimental import pallas as pl
from jax.experimental.pallas import tpu as pltpu
from jax.sharding import PartitionSpec as P

MESH = pl.DeviceIdType.MESH
F32, BF16, I32 = jnp.float32, jnp.bfloat16, jnp.int32
NX, NY, NZ, NC = 4, 4, 8, 2
PER = 8
GROUP = 8
COLS, W = 64, 128
BLOCKS = 256
CAP = 4
UPPER = NY * NZ * NC * 2
NT = (((1,), (1,)), ((), ()))
NN = (((1,), (0,)), ((), ()))


def kernel(
    target_ref, place_ref, right_hbm, upper_right_hbm, inv_hbm, upper_inv_hbm, u_hbm,
    leaf_out, upper_out,
    u, x, inv, lf, t, idx_v, idx_s, a0, r0, o1, r1, o2, r2, ur, ui, us, g, lo,
    loc, xs, xr, cs, cr, ys, yr, zs, zr, azs, azr, ays, ayr, acs, acr,
):
    leaf, rx = lax.axis_index("leaf"), lax.axis_index("rhs")
    y, z, c = leaf // (NZ * NC), (leaf // NC) % NZ, leaf % NC

    def at(yy, zz, cc, xx):
        return ((yy * NZ + zz) * NC + cc, xx)

    def off_x(d):
        return at(y, z, c, (rx + d) % NX)

    def off_y(d):
        return at((y + d) % NY, z, c, rx)

    def off_z(d):
        return at(y, (z + d) % NZ, c, rx)

    sibling = at(y, z, 1 - c, rx)

    def remote(src, dst, ssem, rsem, dev):
        return pltpu.make_async_remote_copy(
            src_ref=src, dst_ref=dst, send_sem=ssem, recv_sem=rsem, device_id=dev, device_id_type=MESH
        )

    own = pltpu.make_async_copy(inv_hbm, inv.at[rx], loc.at[0])
    own.start()
    load_x = pltpu.make_async_copy(right_hbm, x, loc.at[1])
    load_x.start()
    order = (0, 1, 3, 2)
    load_u = []
    for i, d in enumerate(order):
        base = ((rx + NX - d) % NX) * (GROUP * PER)
        load_u.append(pltpu.make_async_copy(u_hbm.at[pl.ds(base, GROUP * PER)], u.at[pl.ds(base, GROUP * PER)], loc.at[2 + i]))
        load_u[-1].start()
    load_ur = pltpu.make_async_copy(upper_right_hbm, ur, loc.at[6])
    load_ur.start()
    load_ui = pltpu.make_async_copy(upper_inv_hbm, ui, loc.at[7])
    load_ui.start()

    barrier = pltpu.get_barrier_semaphore()
    peers = [off_x(d) for d in range(1, NX)] + [off_y(d) for d in range(1, NY)] + [off_z(d) for d in range(1, NZ)] + [sibling]
    for dev in peers:
        pl.semaphore_signal(barrier, inc=1, device_id=dev, device_id_type=MESH)

    lane = lax.broadcasted_iota(I32, (BLOCKS, W), 1)
    row = lax.broadcasted_iota(I32, (BLOCKS, W), 0)
    pos = jnp.sum(jnp.where(target_ref[...] == lane, place_ref[...], 0), axis=1, keepdims=True)
    cand = jnp.where(pos == lane, row, BLOCKS)
    for s in range(CAP):
        low = jnp.min(cand, axis=0, keepdims=True)
        idx_v[s : s + 1, :] = low
        cand = jnp.where(cand > low, cand, BLOCKS)
    where_in_g = ((pos // 2) % 2) * (UPPER // 2) + (pos // 4) * 2 + pos % 2
    for h in range(BLOCKS // W):
        idx_v[CAP + h : CAP + h + 1, :] = jnp.sum(jnp.where(row - h * W == lane, where_in_g, 0), axis=0, keepdims=True)
    idx_v[CAP + 2 :, :] = jnp.zeros((8 - CAP - 2, W), I32)
    to_smem = pltpu.make_async_copy(idx_v, idx_s, loc.at[8])
    to_smem.start()

    pl.semaphore_wait(barrier, len(peers))

    send_x = [remote(inv_hbm, inv.at[rx], xs.at[d - 1], xr.at[d - 1], off_x(d)) for d in (1, 3, 2)]
    for cp in send_x:
        cp.start()
    t[BLOCKS] = jnp.zeros((COLS, W), BF16)
    own.wait()
    load_x.wait()

    def forward(n, _):
        f = lax.dot_general(x[n].astype(BF16), inv[n // GROUP, n % GROUP], NT, preferred_element_type=F32)
        lf[n] = f
        r = lax.dot_general(f.astype(BF16), u[pl.ds(n * PER, PER)].reshape(PER * W, W), NT, preferred_element_type=F32)
        for b in range(PER):
            t[n * PER + b] = r[:, b * W : (b + 1) * W].astype(BF16)
        return 0

    for i, d in enumerate(order):
        src = (rx + NX - d) % NX
        if d:
            remote(inv_hbm, inv.at[src], xs.at[d - 1], xr.at[d - 1], off_x(d)).wait_recv()
        load_u[i].wait()
        lax.fori_loop(src * GROUP, src * GROUP + GROUP, forward, 0)
    to_smem.wait()

    def sum_of(p):
        total = t[idx_s[0, p]].astype(F32)
        for s in range(1, CAP):
            total = total + t[idx_s[s, p]].astype(F32)
        return total

    y_order = (2, 1, 3, 0)

    def place(d, zz, cc, j):
        return ((((y + d) % NY) * NZ + zz) * NC + cc) * 2 + j

    send_c = []
    for j in range(2):
        for d in y_order:
            def to_sibling(zz, _, d=d, j=j):
                a0[j, d, zz] = sum_of(place(d, zz, 1 - c, j)).astype(BF16)
                return 0

            lax.fori_loop(0, NZ, to_sibling, 0)
            cp = remote(a0.at[j, d], r0.at[j, d], cs.at[j, d], cr.at[j, d], sibling)
            cp.start()
            send_c.append(cp)
    send_y = []
    for j in range(2):
        for d in y_order:
            remote(a0.at[j, d], r0.at[j, d], cs.at[j, d], cr.at[j, d], sibling).wait_recv()

            def to_y(zz, _, d=d, j=j):
                o1[j, d, zz] = (sum_of(place(d, zz, c, j)) + r0[j, d, zz].astype(F32)).astype(BF16)
                return 0

            lax.fori_loop(0, NZ, to_y, 0)
            if d:
                cp = remote(o1.at[j, d], r1.at[j, d], ys.at[j, d], yr.at[j, d], off_y(d))
                cp.start()
                send_y.append(cp)
    send_z = []
    for j in range(2):
        for d in (2, 1, 3):
            remote(o1.at[j, d], r1.at[j, d], ys.at[j, d], yr.at[j, d], off_y(d)).wait_recv()
        for dz in (4, 3, 5, 2, 6, 1, 7, 0):
            zz = (z + dz) % NZ
            total = o1[j, 0, zz].astype(F32)
            for d in range(1, NY):
                total = total + r1[j, d, zz].astype(F32)
            o2[j, dz] = total.astype(BF16)
            if dz:
                cp = remote(o2.at[j, dz], r2.at[j, dz], zs.at[j, dz], zr.at[j, dz], off_z(dz))
                cp.start()
                send_z.append(cp)
    load_ur.wait()
    load_ui.wait()
    send_az = []
    mine = (y * NZ + z) * 2
    for j in range(2):
        total = o2[j, 0].astype(F32)
        for dz in range(1, NZ):
            remote(o2.at[j, dz], r2.at[j, dz], zs.at[j, dz], zr.at[j, dz], off_z(dz)).wait_recv()
            total = total + r2[j, dz].astype(F32)
        v = (ur[j] - total).astype(BF16)
        h = lax.dot_general(v, ui[j], NT, preferred_element_type=F32).astype(BF16)
        s = lax.dot_general(h, ui[j], NN, preferred_element_type=F32)
        us[j] = s
        g[c, mine + j] = s.astype(BF16)
    store_us = pltpu.make_async_copy(us, upper_out, loc.at[9])
    store_us.start()
    blk = g.at[c, pl.ds(mine, 2)]
    for dz in (4, 3, 5, 2, 6, 1, 7):
        cp = remote(blk, blk, azs.at[dz], azr.at[dz], off_z(dz))
        cp.start()
        send_az.append(cp)
    send_ay = []
    for dz in (0, 1, 7, 2, 6, 3, 5, 4):
        b = g.at[c, pl.ds((y * NZ + (z + NZ - dz) % NZ) * 2, 2)]
        if dz:
            remote(b, b, azs.at[dz], azr.at[dz], off_z(dz)).wait_recv()
        for d in (2, 1, 3):
            cp = remote(b, b, ays.at[d, dz], ayr.at[d, dz], off_y(d))
            cp.start()
            send_ay.append(cp)
        cp = remote(b, b, acs.at[0, dz], acr.at[0, dz], sibling)
        cp.start()
        send_ay.append(cp)
    for dz in (0, 1, 7, 2, 6, 3, 5, 4):
        for d in (1, 3, 2):
            b = g.at[c, pl.ds((((y + NY - d) % NY) * NZ + (z + NZ - dz) % NZ) * 2, 2)]
            remote(b, b, ays.at[d, dz], ayr.at[d, dz], off_y(d)).wait_recv()
            cp = remote(b, b, acs.at[d, dz], acr.at[d, dz], sibling)
            cp.start()
            send_ay.append(cp)
    for dz in (0, 1, 7, 2, 6, 3, 5, 4):
        for d in range(NY):
            b = g.at[1 - c, pl.ds((((y + NY - d) % NY) * NZ + (z + NZ - dz) % NZ) * 2, 2)]
            remote(b, b, acs.at[d, dz], acr.at[d, dz], sibling).wait_recv()

    def backward(n, _):
        parts = []
        for b in range(PER):
            k = n * PER + b
            e = idx_s[CAP + k // W, k % W]
            parts.append(g[e // (UPPER // 2), e % (UPPER // 2)])
        corr = lax.dot_general(
            jnp.concatenate(parts, axis=1), u[pl.ds(n * PER, PER)].reshape(PER * W, W), NN, preferred_element_type=F32
        )
        back = (lf[n] - corr).astype(BF16)
        lo[n] = lax.dot_general(back, inv[n // GROUP, n % GROUP], NN, preferred_element_type=F32)
        return 0

    stores = []
    for i in range(4):
        lax.fori_loop(i * GROUP, (i + 1) * GROUP, backward, 0)
        part = pl.ds(i * GROUP, GROUP)
        cp = pltpu.make_async_copy(lo.at[part], leaf_out.at[part], loc.at[10 + i])
        cp.start()
        stores.append(cp)
    for cp in send_x + send_c + send_y + send_z + send_az + send_ay:
        cp.wait_send()
    store_us.wait()
    for cp in stores:
        cp.wait()


def on_device(leaf_right, upper_right, leaf_inverse, upper_inverse, update_blocks, block_target, upper_place):
    any_space = pl.BlockSpec(memory_space=pl.ANY)
    vmem = pl.BlockSpec(memory_space=pltpu.VMEM)
    dma = pltpu.SemaphoreType.DMA
    leaves = NX * GROUP
    return pl.pallas_call(
        kernel,
        out_shape=(
            jax.ShapeDtypeStruct((leaves, COLS, W), F32),
            jax.ShapeDtypeStruct((2, COLS, W), F32),
        ),
        in_specs=[vmem, vmem] + [any_space] * 5,
        out_specs=(any_space, any_space),
        scratch_shapes=[
            pltpu.VMEM((BLOCKS, W, W), BF16),
            pltpu.VMEM((leaves, COLS, W), F32),
            pltpu.VMEM((NX, GROUP, W, W), BF16),
            pltpu.VMEM((leaves, COLS, W), F32),
            pltpu.VMEM((BLOCKS + 1, COLS, W), BF16),
            pltpu.VMEM((8, W), I32),
            pltpu.SMEM((8, W), I32),
            pltpu.VMEM((2, NY, NZ, COLS, W), BF16),
            pltpu.VMEM((2, NY, NZ, COLS, W), BF16),
            pltpu.VMEM((2, NY, NZ, COLS, W), BF16),
            pltpu.VMEM((2, NY, NZ, COLS, W), BF16),
            pltpu.VMEM((2, NZ, COLS, W), BF16),
            pltpu.VMEM((2, NZ, COLS, W), BF16),
            pltpu.VMEM((2, COLS, W), F32),
            pltpu.VMEM((2, W, W), BF16),
            pltpu.VMEM((2, COLS, W), F32),
            pltpu.VMEM((2, UPPER // 2, COLS, W), BF16),
            pltpu.VMEM((leaves, COLS, W), F32),
            dma((14,)),
            dma((3,)), dma((3,)),
            dma((2, NY)), dma((2, NY)),
            dma((2, NY)), dma((2, NY)),
            dma((2, NZ)), dma((2, NZ)),
            dma((NZ,)), dma((NZ,)),
            dma((NY, NZ)), dma((NY, NZ)),
            dma((NY, NZ)), dma((NY, NZ)),
        ],
        compiler_params=pltpu.CompilerParams(
            collective_id=0, has_side_effects=True, vmem_limit_bytes=56 * 2**20
        ),
        name="solve",
    )(block_target, upper_place.reshape(1, -1), leaf_right, upper_right, leaf_inverse, upper_inverse, update_blocks)


def solution(mesh):
    return jax.shard_map(
        on_device,
        mesh=mesh,
        in_specs=(
            P("leaf", "rhs", None),
            P("leaf", "rhs", None),
            P(("leaf", "rhs"), None, None),
            P("leaf", None, None),
            P("leaf", None, None),
            P("leaf", None),
            P(),
        ),
        out_specs=(P("leaf", "rhs", None), P("leaf", "rhs", None)),
        check_vma=False,
    )
```

time: 339 us -> 89.7 us (0.26)
  waiting for transfers between devices: 254 us -> 0 us
  Pallas kernels: 0 us -> 83.6 us
  other arithmetic: 40.7 us -> 0 us
  matrix products: 22.3 us -> 0 us
  between operations: 13.8 us -> 0.64 us
    reduce_scatter x1 -> x0, waiting for transfers between devices: 140 us -> none  [on_device(): lax.psum_scatter(jax.ops.segment_sum(updates, local_index, num_segments=u...]
    all_gather x2 -> x0, waiting for transfers between devices: 113 us -> none  [the longest x1 83 us: on_device(): solved_table = lax.all_gather(upper_sent, 'leaf', axis=0, tiled=True)]
    pallas_call x0 -> x1, Pallas kernels: none -> 83.6 us  [on_device(): pl.pallas_call(kernel, out_shape=(jax.ShapeDtypeStruct((leaves, COLS, W),...]
    scatter-add x1 -> x0, other arithmetic: 39.9 us -> none  [on_device(): jax.ops.segment_sum(updates, local_index, num_segments=upper_rows * lax.a...]
    dot_general x5 -> x0, matrix products: 22.3 us -> none  [the longest x1 9.63 us: on_device(): jnp.einsum('ncw,nbvw->nbcv', leaf_half, grouped, preferred_element_type=j...]
    unnamed x6 -> x3, local copies, waits for them, and re-layouts: 0.02 us -> 5.25 us
    gather x1 -> x0, local copies, waits for them, and re-layouts: 4.61 us -> none  [on_device(): chosen = jnp.take(solved_table, position, axis=0)]
  transfers between devices with their start and end apart: 3 -> 0, of which waited for: 3 -> 0; matrix products, arithmetic and copies ran while one was open for 0% -> 0% of each run, Pallas kernels for 0% -> 0%
where the time goes in v1:
time: 89.7 us; the launch traced here: 89.5 us
  Pallas kernels  83.6 us (93%)
  local copies, waits for them, and re-layouts  5.25 us (6%)
    pallas_call x1, Pallas kernels, on_device(): pl.pallas_call(kernel, out_shape=(jax.ShapeDtypeStruct((leaves, COLS, W),...  83.6 us
    unnamed x3, local copies, waits for them, and re-layouts  5.25 us

profile of v1, /device:TPU:1, one launch (start us, length us, event | category | flops | bytes accessed | tf_op | source)
XLA Modules:
  0.0 89.5 jit_solution(13874038554295144166)
XLA Ops:
  0.6 1.5 %copy.9.target_ref = s32[256,1]{1,0:T(8,128)} copy(s32[256,1]{0,1:T(1,128)} %param.12) | data formatting | bytes 2048 | tf_op args[5]
  2.1 83.6 %solve.1 = (f32[32,64,128]{2,1,0:T(8,128)}, f32[2,64,128]{2,1,0:T(8,128)}) custom-call(s32[256,1]{1,0:T(8,128)} %copy.9.target_ref, s32[1,128]{1,0:T(1,128)} %bitcast.1, f32[32,64,128]{2,1,0:T(8,128)} %right_hbm.1, f32[2,64,128]{2,1,0:T(8,128)} %upper_right_hbm.1, bf16[8,128,128]{2,1,0:T(8,128)(2,1)} %inv_hbm.1, bf16[2,128,128]{2,1,0:T(8,128)(2,1)} %upper_inv_hbm.1, ...), custom_call_target="tpu_custom_call" | custom-call | tf_op jit(solution)/shard_map/solve/pallas_call | solution.py:238
  85.7 2.3 %copy.12 = f32[32,64,128]{2,1,0:T(8,128)} copy(f32[32,64,128]{2,1,0:T(8,128)} %get-tuple-element.4) | data formatting | bytes 2097152
  88.0 1.5 %copy.13 = f32[2,64,128]{2,1,0:T(8,128)} copy(f32[2,64,128]{2,1,0:T(8,128)} %get-tuple-element.5) | data formatting | bytes 131072

commit v2 on v0

v2 whole, which is shorter than its diff:
```python
import jax
import jax.numpy as jnp
from jax import lax
from jax.experimental import pallas as pl
from jax.experimental.pallas import tpu as pltpu
from jax.sharding import PartitionSpec as P

MESH = pl.DeviceIdType.MESH
F32, BF16, I32 = jnp.float32, jnp.bfloat16, jnp.int32
NX, NY, NZ, NC = 4, 4, 8, 2
PER = 8
GROUP = 8
COLS, W = 64, 128
BLOCKS = 256
CAP = 4
UPPER = NY * NZ * NC * 2
STRIP = 16
NT = (((1,), (1,)), ((), ()))
NN = (((1,), (0,)), ((), ()))


def kernel(
    target_ref, place_ref, right_hbm, upper_right_hbm, inv_hbm, upper_inv_hbm, u_hbm,
    leaf_out, upper_out,
    u, x, pk, inv, lf, t, idx_v, idx_s, az, ay, bz, by, oz, oy, rzr, rzl, ryr, ryl,
    o2, r2, o3, r3, keep, ur, ui, us, g, lo,
    loc, xs, xr, csz, crz, csy, cry, zs, zr, ys, yr, s2, q2, s3, q3,
    azs, azr, ays, ayr, aws, awr, ars, arr, b1s, b1r, b0s, b0r,
):
    leaf, rx = lax.axis_index("leaf"), lax.axis_index("rhs")
    y, z, c = leaf // (NZ * NC), (leaf // NC) % NZ, leaf % NC

    def at(yy, zz, cc, xx):
        return ((yy * NZ + zz) * NC + cc, xx)

    def off_x(d):
        return at(y, z, c, (rx + d) % NX)

    def off_y(d):
        return at((y + d) % NY, z, c, rx)

    def off_z(d):
        return at(y, (z + d) % NZ, c, rx)

    sibling = at(y, z, 1 - c, rx)
    sends = []

    def remote(src, dst, ssem, rsem, dev):
        return pltpu.make_async_remote_copy(
            src_ref=src, dst_ref=dst, send_sem=ssem, recv_sem=rsem, device_id=dev, device_id_type=MESH
        )

    def send(src, dst, ssem, rsem, dev):
        cp = remote(src, dst, ssem, rsem, dev)
        cp.start()
        sends.append(cp)

    def arrived(ref, ssem, rsem, dev):
        remote(ref, ref, ssem, rsem, dev).wait_recv()

    own = pltpu.make_async_copy(inv_hbm, inv.at[rx], loc.at[0])
    own.start()

    def piece(i):
        d = jnp.where(i < 2, 0, jnp.where(i >= 6, 2, 1 + 2 * (i % 2)))
        half = jnp.where((i == 4) | (i == 5), 1 - i % 2, i % 2)
        return (rx + NX - d) % NX, half

    def load_u(i):
        src, half = piece(i)
        part = pl.ds((src * 2 + half) * (4 * PER), 4 * PER)
        return pltpu.make_async_copy(u_hbm.at[part], u.at[part], loc.at[1 + i])

    load_x = pltpu.make_async_copy(right_hbm, x, loc.at[9])
    load_x.start()

    def start_u(i, _):
        load_u(i).start()
        return 0

    lax.fori_loop(0, 8, start_u, 0)
    load_ur = pltpu.make_async_copy(upper_right_hbm, ur, loc.at[10])
    load_ur.start()
    load_ui = pltpu.make_async_copy(upper_inv_hbm, ui, loc.at[11])
    load_ui.start()

    barrier = pltpu.get_barrier_semaphore()
    peers = [off_x(1), off_x(3)] + [off_y(d) for d in range(1, NY)] + [off_z(d) for d in range(1, NZ)] + [sibling]
    for dev in peers:
        pl.semaphore_signal(barrier, inc=1, device_id=dev, device_id_type=MESH)

    lane = lax.broadcasted_iota(I32, (BLOCKS, W), 1)
    row = lax.broadcasted_iota(I32, (BLOCKS, W), 0)
    target = jnp.concatenate(
        [
            jnp.sum(jnp.where(lane[:W] == row[:W], target_ref[:, h * W : (h + 1) * W], 0), axis=1, keepdims=True)
            for h in range(BLOCKS // W)
        ],
        axis=0,
    )
    pos = jnp.sum(jnp.where(target == lane, place_ref[...], 0), axis=1, keepdims=True)
    cand = jnp.where(pos == lane, row, BLOCKS)
    for s in range(CAP):
        low = jnp.min(cand, axis=0, keepdims=True)
        idx_v[s : s + 1, :] = low
        cand = jnp.where(cand > low, cand, BLOCKS)
    where_in_g = (((pos // 2) % 2) * 2 + pos % 2) * (UPPER // 4) + ((pos // 4) % NZ) * NY + pos // (4 * NZ)
    for h in range(BLOCKS // W):
        idx_v[CAP + h : CAP + h + 1, :] = jnp.sum(jnp.where(row - h * W == lane, where_in_g, 0), axis=0, keepdims=True)
    idx_v[CAP + 2 :, :] = jnp.zeros((8 - CAP - 2, W), I32)
    to_smem = pltpu.make_async_copy(idx_v, idx_s, loc.at[12])
    to_smem.start()

    own.wait()
    lane16 = lax.broadcasted_iota(I32, (STRIP, W), 1)

    def strip(n, s):
        return inv[rx, n, s * STRIP : (s + 1) * STRIP, :].astype(F32)

    for h in range(2):
        for q in range(2):
            two = (h * 4 + q * 2, h * 4 + q * 2 + 1)
            for m, n in enumerate(two):
                for s in range(3):
                    pk[rx, h, q, m * 3 + s] = (strip(n, 6 - s) + pltpu.roll(strip(n, s), STRIP * (7 - s), 1)).astype(BF16)
                pk[rx, h, q, 6 + m] = inv[rx, n, 7 * STRIP :, :]
            pk[rx, h, q, 8] = (strip(two[0], 3) + pltpu.roll(strip(two[1], 3), W // 2, 1)).astype(BF16)

    pl.semaphore_wait(barrier, len(peers))

    mine_x = [pk.at[rx, 0], pk.at[rx, 1]]
    for h, i, d in ((0, 2, 1), (1, 3, 3), (1, 4, 1), (0, 5, 3)):
        send(mine_x[h], mine_x[h], xs.at[i], xr.at[i], off_x(d))
    relay_right, relay_left = pk.at[(rx + 3) % NX, 0], pk.at[(rx + 1) % NX, 1]
    relays = (
        remote(relay_right, relay_right, xs.at[6], xr.at[6], off_x(1)),
        remote(relay_left, relay_left, xs.at[7], xr.at[7], off_x(3)),
    )
    sends.extend(relays)
    t[BLOCKS] = jnp.zeros((COLS, W), F32)
    load_x.wait()

    def forward(i, _):
        src, half = piece(i)

        @pl.when(i >= 2)
        def _():
            arrived(pk.at[src, half], xs.at[i], xr.at[i], off_x(1))

            @pl.when(i == 2)
            def _():
                relays[0].start()

            @pl.when(i == 3)
            def _():
                relays[1].start()

            for q in range(2):
                for m in range(2):
                    n = half * 4 + q * 2 + m
                    for s in range(3):
                        both = pk[src, half, q, m * 3 + s].astype(F32)
                        cut = STRIP * (7 - s)
                        inv[src, n, (6 - s) * STRIP : (7 - s) * STRIP, :] = jnp.where(lane16 < cut, both, 0.0).astype(BF16)
                        inv[src, n, s * STRIP : (s + 1) * STRIP, :] = jnp.where(
                            lane16 < W - cut, pltpu.roll(both, W - cut, 1), 0.0
                        ).astype(BF16)
                    inv[src, n, 7 * STRIP :, :] = pk[src, half, q, 6 + m]
                    both = pk[src, half, q, 8].astype(F32)
                    if m:
                        both = pltpu.roll(both, W // 2, 1)
                    inv[src, n, 3 * STRIP : 4 * STRIP, :] = jnp.where(lane16 < W // 2, both, 0.0).astype(BF16)

        load_u(i).wait()
        base = src * GROUP + half * 4
        solved = []
        for q in range(4):
            f = lax.dot_general(x[base + q].astype(BF16), inv[src, half * 4 + q], NT, preferred_element_type=F32)
            lf[base + q] = f
            solved.append(f.astype(BF16))
        for q in range(4):
            n = base + q
            r = lax.dot_general(solved[q], u[pl.ds(n * PER, PER)].reshape(PER * W, W), NT, preferred_element_type=F32)
            for b in range(PER):
                t[n * PER + b] = r[:, b * W : (b + 1) * W]
        return 0

    lax.fori_loop(0, 8, forward, 0)
    to_smem.wait()

    def sum_of(p):
        return (t[idx_s[0, p]] + t[idx_s[1, p]]) + (t[idx_s[2, p]] + t[idx_s[3, p]])

    def at_z(d, yy, cc):
        return ((yy * NZ + (z + d) % NZ) * NC + cc) * 2

    def at_y(d, zz, cc):
        return ((((y + d) % NY) * NZ + zz) * NC + cc) * 2 + 1

    def sib_z(d):
        def body(k, _):
            az[d, k] = sum_of(at_z(d, k, 1 - c)).astype(BF16)
            return 0

        lax.fori_loop(0, NY, body, 0, unroll=True)
        send(az.at[d], bz.at[d], csz.at[d], crz.at[d], sibling)

    def sib_y(d):
        def body(k, _):
            ay[d, k] = sum_of(at_y(d, k, 1 - c)).astype(BF16)
            return 0

        lax.fori_loop(0, NZ, body, 0, unroll=4)
        send(ay.at[d], by.at[d], csy.at[d], cry.at[d], sibling)

    sib_z(4), sib_y(2), sib_z(3), sib_z(5), sib_y(1), sib_y(3)
    sib_z(2), sib_z(6), sib_z(1), sib_z(7), sib_y(0), sib_z(0)

    def has_z(d):
        arrived(bz.at[d], csz.at[d], crz.at[d], sibling)

    def has_y(d):
        arrived(by.at[d], csy.at[d], cry.at[d], sibling)

    def sum_z(d, k):
        return sum_of(at_z(d, k, c)) + bz[d, k].astype(F32)

    def sum_y(d, k):
        return sum_of(at_y(d, k, c)) + by[d, k].astype(F32)

    zr_dev, zl_dev, yr_dev, yl_dev = off_z(1), off_z(NZ - 1), off_y(1), off_y(NY - 1)

    has_z(4)
    for k in range(NY):
        oz[4, k] = sum_z(4, k).astype(BF16)
    lower, upper = pl.ds(0, 2), pl.ds(2, 2)
    send(oz.at[4, lower], rzr.at[0, lower], zs.at[0, 0], zr.at[0, 0], zr_dev)
    send(oz.at[4, upper], rzl.at[0, upper], zs.at[1, 0], zr.at[1, 0], zl_dev)
    has_y(2)

    def first_y(k, _):
        oy[2, k] = sum_y(2, k).astype(BF16)
        return 0

    lax.fori_loop(0, NZ, first_y, 0, unroll=4)
    low4, high4 = pl.ds(0, 4), pl.ds(4, 4)
    send(oy.at[2, low4], ryr.at[0, low4], ys.at[0, 0], yr.at[0, 0], yr_dev)
    send(oy.at[2, high4], ryl.at[0, high4], ys.at[1, 0], yr.at[1, 0], yl_dev)

    def z_step(s):
        for way, d, got, dev in ((0, 5 - s, rzr, zr_dev), (1, 3 + s, rzl, zl_dev)):
            has_z(d)
            part = got.at[s - 2] if s > 2 else got.at[0, lower if way == 0 else upper]
            arrived(part, zs.at[way, s - 2], zr.at[way, s - 2], dev)
            for k in range(NY):
                v = sum_z(d, k)
                if s > 2 or (k < 2) == (way == 0):
                    v = v + got[s - 2, k].astype(F32)
                oz[d, k] = v.astype(BF16)
            send(oz.at[d], got.at[s - 1], zs.at[way, s - 1], zr.at[way, s - 1], dev)

    z_step(2)
    for way, d, got, dev, part in ((0, 1, ryr, yr_dev, low4), (1, 3, ryl, yl_dev, high4)):
        has_y(d)
        arrived(got.at[0, part], ys.at[way, 0], yr.at[way, 0], dev)

        def with_got(k, _, d=d, got=got):
            oy[d, k] = (sum_y(d, k) + got[0, k].astype(F32)).astype(BF16)
            return 0

        def without(k, _, d=d):
            oy[d, k] = sum_y(d, k).astype(BF16)
            return 0

        for h in range(2):
            lax.fori_loop(4 * h, 4 * h + 4, with_got if h == way else without, 0, unroll=True)
        send(oy.at[d], got.at[1], ys.at[way, 1], yr.at[way, 1], dev)
    z_step(3)
    z_step(4)

    has_y(0)
    arrived(ryr.at[1], ys.at[0, 1], yr.at[0, 1], yr_dev)
    arrived(ryl.at[1], ys.at[1, 1], yr.at[1, 1], yl_dev)
    for d in (4, 3, 5, 2, 6, 1, 7, 0):
        k = (z + d) % NZ
        v = sum_y(0, k) + ryr[1, k].astype(F32) + ryl[1, k].astype(F32)
        if d:
            o2[d] = v.astype(BF16)
            send(o2.at[d], r2.at[d], s2.at[d], q2.at[d], off_z(d))
        else:
            keep[1] = v
    has_z(0)
    arrived(rzr.at[3], zs.at[0, 3], zr.at[0, 3], zr_dev)
    arrived(rzl.at[3], zs.at[1, 3], zr.at[1, 3], zl_dev)
    for d in (2, 1, 3, 0):
        k = (y + d) % NY
        v = sum_z(0, k) + rzr[3, k].astype(F32) + rzl[3, k].astype(F32)
        if d:
            o3[d] = v.astype(BF16)
            send(o3.at[d], r3.at[d], s3.at[d], q3.at[d], off_y(d))
        else:
            keep[0] = v
    load_ur.wait()
    load_ui.wait()

    def blk(j, zz, yy, n=1):
        return g.at[pl.ds((c * 2 + j) * (UPPER // 4) + ((zz + NZ) % NZ) * NY + (yy + NY) % NY, n)]

    def solve(j, total):
        v = (ur[j] - total).astype(BF16)
        h = lax.dot_general(v, ui[j], NT, preferred_element_type=F32).astype(BF16)
        s = lax.dot_general(h, ui[j], NN, preferred_element_type=F32)
        us[j] = s
        g[(c * 2 + j) * (UPPER // 4) + z * NY + y] = s.astype(BF16)

    def out1(d):
        b = blk(1, z - d, y)
        send(b, b, ays.at[0, d], ayr.at[0, d], yr_dev)
        send(b, b, ays.at[1, d], ayr.at[1, d], yl_dev)
        send(b, b, b1s.at[0, d], b1r.at[0, d], sibling)

    total = keep[1]
    for d in (1, 7, 2, 6, 3, 5, 4):
        arrived(r2.at[d], s2.at[d], q2.at[d], off_z(d))
        total = total + r2[d].astype(F32)
    solve(1, total)
    b = blk(1, z, y)
    for d in (4, 3, 5, 2, 6, 1, 7):
        send(b, b, azs.at[d], azr.at[d], off_z(d))
    out1(0)

    total = keep[0]
    for d in (1, 3, 2):
        arrived(r3.at[d], s3.at[d], q3.at[d], off_y(d))
        total = total + r3[d].astype(F32)
    solve(0, total)
    b = blk(0, z, y)
    for d in (2, 1, 3):
        send(b, b, aws.at[d], awr.at[d], off_y(d))
    store_us = pltpu.make_async_copy(us, upper_out, loc.at[13])
    store_us.start()

    def in1(d):
        b = blk(1, z - d, y)
        arrived(b, azs.at[d], azr.at[d], off_z(d))
        out1(d)

    halves = {0: 0, 1: 1, 7: 0, 2: 1, 6: 0, 3: 1, 5: 0, 4: 1}

    def along_y(d):
        for way, dy, dev in ((0, -1, yr_dev), (1, 1, yl_dev)):
            b = blk(1, z - d, y + dy)
            arrived(b, ays.at[way, d], ayr.at[way, d], dev)
            if halves[d] == way:
                send(b, b, ays.at[2, d], ayr.at[2, d], dev)
            send(b, b, b1s.at[1 + way, d], b1r.at[1 + way, d], sibling)

    def last_y(d):
        b = blk(1, z - d, y + 2)
        arrived(b, ays.at[2, d], ayr.at[2, d], yr_dev)
        send(b, b, b1s.at[3, d], b1r.at[3, d], sibling)

    def ring_piece(way, k):
        s = k // 2 + 1
        return blk(0, z - s if way == 0 else z + s, 2 * (k % 2 if way == 0 else 1 - k % 2), 2)

    def along_z(k):
        for way, dev in ((0, zr_dev), (1, zl_dev)):
            b = ring_piece(way, k)
            arrived(b, ars.at[way, k], arr.at[way, k], dev)
            if k <= 4:
                send(b, b, ars.at[way, k + 2], arr.at[way, k + 2], dev)
            send(b, b, b0s.at[way, k], b0r.at[way, k], sibling)

    for d in (1, 3, 2):
        b = blk(0, z, y - d)
        arrived(b, aws.at[d], awr.at[d], off_y(d))
    for k in range(2):
        for way, dev in ((0, zr_dev), (1, zl_dev)):
            b = blk(0, z, 2 * (k if way == 0 else 1 - k), 2)
            send(b, b, ars.at[way, k], arr.at[way, k], dev)
    b = blk(0, z, 0, NY)
    send(b, b, b0s.at[0, 7], b0r.at[0, 7], sibling)
    in1(1), in1(7), along_y(0), in1(2), in1(6), along_y(1), along_y(7)
    along_z(0), in1(3), in1(5), along_z(1), along_y(2), along_y(6), in1(4), along_z(2)
    along_y(3), along_y(5), along_z(3), along_y(4), along_z(4)
    for d in (0, 1, 7, 2, 6, 3, 5, 4):
        last_y(d)
    along_z(5), along_z(6)

    def there(j, zz, yy, n=1):
        return g.at[pl.ds(((1 - c) * 2 + j) * (UPPER // 4) + ((zz + NZ) % NZ) * NY + (yy + NY) % NY, n)]

    for d in range(NZ):
        for kind, dy in ((0, 0), (1, -1), (2, 1), (3, 2)):
            arrived(there(1, z - d, y + dy), b1s.at[kind, d], b1r.at[kind, d], sibling)
    arrived(there(0, z, 0, NY), b0s.at[0, 7], b0r.at[0, 7], sibling)
    for k in range(7):
        for way in range(2):
            s = k // 2 + 1
            b = there(0, z - s if way == 0 else z + s, 2 * (k % 2 if way == 0 else 1 - k % 2), 2)
            arrived(b, b0s.at[way, k], b0r.at[way, k], sibling)

    def backward(i, _):
        for q in range(4):
            n = i * 4 + q
            parts = []
            for b in range(PER):
                k = n * PER + b
                parts.append(g[idx_s[CAP + k // W, k % W]])
            corr = lax.dot_general(
                jnp.concatenate(parts, axis=1), u[pl.ds(n * PER, PER)].reshape(PER * W, W), NN, preferred_element_type=F32
            )
            back = (lf[n] - corr).astype(BF16)
            lo[n] = lax.dot_general(back, inv[n // GROUP, n % GROUP], NN, preferred_element_type=F32)
        return 0

    stores = []
    for i in range(4):
        lax.fori_loop(i * 2, i * 2 + 2, backward, 0)
        part = pl.ds(i * GROUP, GROUP)
        cp = pltpu.make_async_copy(lo.at[part], leaf_out.at[part], loc.at[14 + i])
        cp.start()
        stores.append(cp)
    for cp in sends:
        cp.wait_send()
    store_us.wait()
    for cp in stores:
        cp.wait()


def on_device(leaf_right, upper_right, leaf_inverse, upper_inverse, update_blocks, block_target, upper_place):
    any_space = pl.BlockSpec(memory_space=pl.ANY)
    vmem = pl.BlockSpec(memory_space=pltpu.VMEM)
    dma = pltpu.SemaphoreType.DMA
    leaves = NX * GROUP
    half = lambda *shape: pltpu.VMEM(shape + (COLS, W), BF16)
    wide = lambda *shape: pltpu.VMEM(shape + (COLS, W), F32)
    return pl.pallas_call(
        kernel,
        out_shape=(
            jax.ShapeDtypeStruct((leaves, COLS, W), F32),
            jax.ShapeDtypeStruct((2, COLS, W), F32),
        ),
        in_specs=[vmem, vmem] + [any_space] * 5,
        out_specs=(any_space, any_space),
        scratch_shapes=[
            pltpu.VMEM((BLOCKS, W, W), BF16),
            wide(leaves),
            pltpu.VMEM((NX, 2, 2, 9, STRIP, W), BF16),
            pltpu.VMEM((NX, GROUP, W, W), BF16),
            wide(leaves),
            wide(BLOCKS + 1),
            pltpu.VMEM((8, W), I32),
            pltpu.SMEM((8, W), I32),
            half(NZ, NY), half(NY, NZ),
            half(NZ, NY), half(NY, NZ),
            half(NZ, NY), half(NY, NZ),
            half(4, NY), half(4, NY),
            half(2, NZ), half(2, NZ),
            half(NZ), half(NZ),
            half(NY), half(NY),
            wide(2),
            wide(2),
            pltpu.VMEM((2, W, W), BF16),
            wide(2),
            half(UPPER),
            wide(leaves),
            dma((18,)),
            dma((8,)), dma((8,)),
            dma((NZ,)), dma((NZ,)), dma((NY,)), dma((NY,)),
            dma((2, 4)), dma((2, 4)), dma((2, 2)), dma((2, 2)),
            dma((NZ,)), dma((NZ,)), dma((NY,)), dma((NY,)),
            dma((NZ,)), dma((NZ,)),
            dma((3, NZ)), dma((3, NZ)),
            dma((NY,)), dma((NY,)),
            dma((2, 7)), dma((2, 7)),
            dma((4, NZ)), dma((4, NZ)),
            dma((2, 8)), dma((2, 8)),
        ],
        compiler_params=pltpu.CompilerParams(
            collective_id=0, has_side_effects=True, vmem_limit_bytes=56 * 2**20
        ),
        name="solve",
    )(block_target.reshape(1, -1), upper_place.reshape(1, -1), leaf_right, upper_right, leaf_inverse, upper_inverse, update_blocks)


def solution(mesh):
    return jax.shard_map(
        on_device,
        mesh=mesh,
        in_specs=(
            P("leaf", "rhs", None),
            P("leaf", "rhs", None),
            P(("leaf", "rhs"), None, None),
            P("leaf", None, None),
            P("leaf", None, None),
            P("leaf", None),
            P(),
        ),
        out_specs=(P("leaf", "rhs", None), P("leaf", "rhs", None)),
        check_vma=False,
    )
```

time: 339 us -> 72.1 us (0.21)
  waiting for transfers between devices: 254 us -> 0 us
  Pallas kernels: 0 us -> 67.5 us
  other arithmetic: 40.7 us -> 0 us
  matrix products: 22.3 us -> 0 us
  between operations: 13.8 us -> 0.64 us
    reduce_scatter x1 -> x0, waiting for transfers between devices: 140 us -> none  [on_device(): lax.psum_scatter(jax.ops.segment_sum(updates, local_index, num_segments=u...]
    all_gather x2 -> x0, waiting for transfers between devices: 113 us -> none  [the longest x1 83 us: on_device(): solved_table = lax.all_gather(upper_sent, 'leaf', axis=0, tiled=True)]
    pallas_call x0 -> x1, Pallas kernels: none -> 67.5 us  [on_device(): pl.pallas_call(kernel, out_shape=(jax.ShapeDtypeStruct((leaves, COLS, W),...]
    scatter-add x1 -> x0, other arithmetic: 39.9 us -> none  [on_device(): jax.ops.segment_sum(updates, local_index, num_segments=upper_rows * lax.a...]
    dot_general x5 -> x0, matrix products: 22.3 us -> none  [the longest x1 9.63 us: on_device(): jnp.einsum('ncw,nbvw->nbcv', leaf_half, grouped, preferred_element_type=j...]
    gather x1 -> x0, local copies, waits for them, and re-layouts: 4.61 us -> none  [on_device(): chosen = jnp.take(solved_table, position, axis=0)]
    unnamed x6 -> x2, local copies, waits for them, and re-layouts: 0.02 us -> 3.78 us
  transfers between devices with their start and end apart: 3 -> 0, of which waited for: 3 -> 0; matrix products, arithmetic and copies ran while one was open for 0% -> 0% of each run, Pallas kernels for 0% -> 0%
where the time goes in v2:
time: 72.1 us; the launch traced here: 71.9 us
  Pallas kernels  67.5 us (94%)
  local copies, waits for them, and re-layouts  3.78 us (5%)
    pallas_call x1, Pallas kernels, on_device(): pl.pallas_call(kernel, out_shape=(jax.ShapeDtypeStruct((leaves, COLS, W),...  67.5 us
    unnamed x2, local copies, waits for them, and re-layouts  3.78 us

profile of v2, /device:TPU:1, one launch (start us, length us, event | category | flops | bytes accessed | tf_op | source)
XLA Modules:
  0.0 71.9 jit_solution(15676214843202192884)
XLA Ops:
  0.6 67.5 %solve.1 = (f32[32,64,128]{2,1,0:T(8,128)}, f32[2,64,128]{2,1,0:T(8,128)}) custom-call(s32[1,256]{1,0:T(1,128)} %bitcast.2, s32[1,128]{1,0:T(1,128)} %bitcast.3, f32[32,64,128]{2,1,0:T(8,128)} %right_hbm.1, f32[2,64,128]{2,1,0:T(8,128)} %upper_right_hbm.1, bf16[8,128,128]{2,1,0:T(8,128)(2,1)} %inv_hbm.1, bf16[2,128,128]{2,1,0:T(8,128)(2,1)} %upper_inv_hbm.1, ...), custom_call_target="tpu_custom_call" | custom-call | tf_op jit(solution)/shard_map/solve/pallas_call | solution.py:439
  68.1 2.3 %copy.11 = f32[32,64,128]{2,1,0:T(8,128)} copy(f32[32,64,128]{2,1,0:T(8,128)} %get-tuple-element.4) | data formatting | bytes 2097152
  70.4 1.5 %copy.12 = f32[2,64,128]{2,1,0:T(8,128)} copy(f32[2,64,128]{2,1,0:T(8,128)} %get-tuple-element.5) | data formatting | bytes 131072

commit v3 on v2

v3 whole, which is shorter than its diff:
```python
import jax
import jax.numpy as jnp
from jax import lax
from jax.experimental import pallas as pl
from jax.experimental.pallas import tpu as pltpu
from jax.sharding import PartitionSpec as P

MESH = pl.DeviceIdType.MESH
F32, BF16, I32 = jnp.float32, jnp.bfloat16, jnp.int32
NX, NY, NZ, NC = 4, 4, 8, 2
PER = 8
GROUP = 8
COLS, W = 64, 128
BLOCKS = 256
CAP = 4
UPPER = NY * NZ * NC * 2
STRIP = 16
NT = (((1,), (1,)), ((), ()))
NN = (((1,), (0,)), ((), ()))


def kernel(
    target_ref, place_ref, right_hbm, upper_right_hbm, inv_hbm, upper_inv_hbm, u_hbm,
    lo, us,
    u, x, pk, inv, lf, t, idx_v, idx_s, az, ay, bz, by, oz, oy, rz, ry,
    o2, r2, o3, r3, keep, ur, ui, g,
    loc, xs, xr, csz, crz, csy, cry, zs, zr, ys, yr, s2, q2, s3, q3,
    azs, azr, ays, ayr, aws, awr, ars, arr, b1s, b1r, b0s, b0r, ready,
):
    leaf, rx = lax.axis_index("leaf"), lax.axis_index("rhs")
    y, z, c = leaf // (NZ * NC), (leaf // NC) % NZ, leaf % NC

    def at(yy, zz, cc, xx):
        return ((yy * NZ + zz) * NC + cc, xx)

    def off_x(d):
        return at(y, z, c, (rx + d) % NX)

    def off_y(d):
        return at((y + d) % NY, z, c, rx)

    def off_z(d):
        return at(y, (z + d) % NZ, c, rx)

    sibling = at(y, z, 1 - c, rx)
    sends = []

    def remote(src, dst, ssem, rsem, dev):
        return pltpu.make_async_remote_copy(
            src_ref=src, dst_ref=dst, send_sem=ssem, recv_sem=rsem, device_id=dev, device_id_type=MESH
        )

    def send(src, dst, ssem, rsem, dev):
        cp = remote(src, dst, ssem, rsem, dev)
        cp.start()
        sends.append(cp)

    def arrived(ref, ssem, rsem, dev):
        remote(ref, ref, ssem, rsem, dev).wait_recv()

    own = pltpu.make_async_copy(inv_hbm, inv.at[rx], loc.at[0])
    own.start()

    def pair_of(i, m):
        d = jnp.where(i < 2, 0, jnp.where(i >= 6, 2, 1 + 2 * (i % 2)))
        half = jnp.where(i >= 6, m, jnp.where((i == 4) | (i == 5), 1 - i % 2, i % 2))
        return (rx + NX - d) % NX, half, jnp.where(i >= 6, i % 2, m)

    def load_u(i, m):
        src, half, q = pair_of(i, m)
        part = pl.ds((src * 4 + half * 2 + q) * (2 * PER), 2 * PER)
        return pltpu.make_async_copy(u_hbm.at[part], u.at[part], loc.at[16 + 2 * i + m])

    load_x = pltpu.make_async_copy(right_hbm, x, loc.at[9])
    load_x.start()

    def start_u(i, _):
        load_u(i, 0).start()
        load_u(i, 1).start()
        return 0

    lax.fori_loop(0, 8, start_u, 0)
    load_ur = pltpu.make_async_copy(upper_right_hbm, ur, loc.at[10])
    load_ur.start()
    load_ui = pltpu.make_async_copy(upper_inv_hbm, ui, loc.at[11])
    load_ui.start()

    barrier = pltpu.get_barrier_semaphore()
    peers = [off_x(1), off_x(3)] + [off_y(1), off_y(3), off_z(1), off_z(7), sibling]
    for dev in peers:
        pl.semaphore_signal(barrier, inc=1, device_id=dev, device_id_type=MESH)

    lane = lax.broadcasted_iota(I32, (BLOCKS, W), 1)
    row = lax.broadcasted_iota(I32, (BLOCKS, W), 0)
    target = jnp.concatenate(
        [
            jnp.sum(jnp.where(lane[:W] == row[:W], target_ref[:, h * W : (h + 1) * W], 0), axis=1, keepdims=True)
            for h in range(BLOCKS // W)
        ],
        axis=0,
    )
    pos = jnp.sum(jnp.where(target == lane, place_ref[...], 0), axis=1, keepdims=True)
    cand = jnp.where(pos == lane, row, BLOCKS)
    for s in range(CAP):
        low = jnp.min(cand, axis=0, keepdims=True)
        idx_v[s : s + 1, :] = low
        cand = jnp.where(cand > low, cand, BLOCKS)
    where_in_g = (((pos // 2) % 2) * 2 + pos % 2) * (UPPER // 4) + ((pos // 4) % NZ) * NY + pos // (4 * NZ)
    for h in range(BLOCKS // W):
        idx_v[CAP + h : CAP + h + 1, :] = jnp.sum(jnp.where(row - h * W == lane, where_in_g, 0), axis=0, keepdims=True)
    idx_v[CAP + 2 :, :] = jnp.zeros((8 - CAP - 2, W), I32)
    to_smem = pltpu.make_async_copy(idx_v, idx_s, loc.at[12])
    to_smem.start()

    own.wait()
    lane16 = lax.broadcasted_iota(I32, (STRIP, W), 1)

    def strip(n, s):
        return inv[rx, n, s * STRIP : (s + 1) * STRIP, :].astype(F32)

    for h in range(2):
        for q in range(2):
            two = (h * 4 + q * 2, h * 4 + q * 2 + 1)
            for m, n in enumerate(two):
                for s in range(3):
                    pk[rx, h, q, m * 3 + s] = (strip(n, 6 - s) + pltpu.roll(strip(n, s), STRIP * (7 - s), 1)).astype(BF16)
                pk[rx, h, q, 6 + m] = inv[rx, n, 7 * STRIP :, :]
            pk[rx, h, q, 8] = (strip(two[0], 3) + pltpu.roll(strip(two[1], 3), W // 2, 1)).astype(BF16)

    pl.semaphore_wait(barrier, len(peers))

    def pass_on(i):
        for d in (1, NZ - 1):
            pl.semaphore_signal(ready.at[i], inc=1, device_id=off_z(d), device_id_type=MESH)

    pass_on(0)
    for d in (1, NY - 1):
        pl.semaphore_signal(ready.at[3], inc=1, device_id=off_y(d), device_id_type=MESH)

    for h, i, d in ((0, 2, 1), (1, 3, 3), (1, 4, 1), (0, 5, 3)):
        for q in range(2):
            b = pk.at[rx, h, q]
            send(b, b, xs.at[i, q], xr.at[i, q], off_x(d))
    relays = []
    for h, d in ((0, 1), (1, 3)):
        for q in range(2):
            b = pk.at[(rx + NX - d) % NX, h, q]
            relays.append(remote(b, b, xs.at[6 + q, h], xr.at[6 + q, h], off_x(d)))
    sends.extend(relays)
    t[BLOCKS] = jnp.zeros((COLS, W), F32)
    load_x.wait()

    def forward(i, _):
        @pl.when(i >= 2)
        def _():
            for m in range(2):
                src, half, q = pair_of(i, m)
                arrived(pk.at[src, half, q], xs.at[i, m], xr.at[i, m], off_x(1))
                for h in range(2):

                    @pl.when(i == 2 + h)
                    def _():
                        relays[2 * h + m].start()

            for k in range(2):

                @pl.when(i == 3 + 2 * k)
                def _():
                    pl.semaphore_wait(ready.at[k], 2)
                    pass_on(k + 1)

            for m in range(2):
                src, half, q = pair_of(i, m)
                for e in range(2):
                    n = half * 4 + q * 2 + e
                    for s in range(3):
                        both = pk[src, half, q, e * 3 + s].astype(F32)
                        cut = STRIP * (7 - s)
                        inv[src, n, (6 - s) * STRIP : (7 - s) * STRIP, :] = jnp.where(lane16 < cut, both, 0.0).astype(BF16)
                        inv[src, n, s * STRIP : (s + 1) * STRIP, :] = jnp.where(
                            lane16 < W - cut, pltpu.roll(both, W - cut, 1), 0.0
                        ).astype(BF16)
                    inv[src, n, 7 * STRIP :, :] = pk[src, half, q, 6 + e]
                    both = pk[src, half, q, 8].astype(F32)
                    if e:
                        both = pltpu.roll(both, W // 2, 1)
                    inv[src, n, 3 * STRIP : 4 * STRIP, :] = jnp.where(lane16 < W // 2, both, 0.0).astype(BF16)

        solved = []
        for m in range(2):
            src, half, q = pair_of(i, m)
            load_u(i, m).wait()
            for e in range(2):
                within = half * 4 + q * 2 + e
                n = src * GROUP + within
                f = lax.dot_general(x[n].astype(BF16), inv[src, within], NT, preferred_element_type=F32)
                lf[n] = f
                solved.append((n, f.astype(BF16)))
        for n, f in solved:
            r = lax.dot_general(f, u[pl.ds(n * PER, PER)].reshape(PER * W, W), NT, preferred_element_type=F32)
            for b in range(PER):
                t[n * PER + b] = r[:, b * W : (b + 1) * W]
        return 0

    lax.fori_loop(0, 8, forward, 0)
    to_smem.wait()
    pl.semaphore_wait(ready.at[2], 2)
    pl.semaphore_wait(ready.at[3], 2)

    def sum_of(p):
        return (t[idx_s[0, p]] + t[idx_s[1, p]]) + (t[idx_s[2, p]] + t[idx_s[3, p]])

    def at_z(d, yy, cc):
        return ((yy * NZ + (z + d) % NZ) * NC + cc) * 2

    def at_y(d, zz, cc):
        return ((((y + d) % NY) * NZ + zz) * NC + cc) * 2 + 1

    def sib_z(d):
        def body(k, _):
            az[d, k] = sum_of(at_z(d, k, 1 - c)).astype(BF16)
            return 0

        lax.fori_loop(0, NY, body, 0, unroll=True)
        send(az.at[d], bz.at[d], csz.at[d], crz.at[d], sibling)

    def sib_y(d):
        def body(k, _):
            ay[d, k] = sum_of(at_y(d, k, 1 - c)).astype(BF16)
            return 0

        lax.fori_loop(0, NZ, body, 0, unroll=4)
        send(ay.at[d], by.at[d], csy.at[d], cry.at[d], sibling)

    def has_z(d):
        arrived(bz.at[d], csz.at[d], crz.at[d], sibling)

    def has_y(d):
        arrived(by.at[d], csy.at[d], cry.at[d], sibling)

    def sum_z(d, k):
        return sum_of(at_z(d, k, c)) + bz[d, k].astype(F32)

    def sum_y(d, k):
        return sum_of(at_y(d, k, c)) + by[d, k].astype(F32)

    lower, upper = pl.ds(0, 2), pl.ds(2, 2)

    def own_z(d, more=()):
        has_z(d)
        for k in range(NY):
            v = sum_z(d, k)
            for got, used in more:
                if k in used:
                    v = v + rz[got, k].astype(F32)
            oz[d, k] = v.astype(BF16)

    def along(kind, d, way, to, part=None):
        a, b = oz.at[d], rz.at[way * 4 + kind]
        if part is not None:
            a, b = oz.at[d, part], rz.at[way * 4 + kind, part]
        send(a, b, zs.at[way, kind], zr.at[way, kind], off_z(to))

    def wait_z(kind, way, part=None):
        b = rz.at[way * 4 + kind] if part is None else rz.at[way * 4 + kind, part]
        arrived(b, zs.at[way, kind], zr.at[way, kind], off_z(1))

    def own_y(d):
        has_y(d)

        def body(k, _):
            oy[d, k] = sum_y(d, k).astype(BF16)
            return 0

        lax.fori_loop(0, NZ, body, 0, unroll=4)
        send(oy.at[d], ry.at[d], ys.at[d], yr.at[d], off_y(d))

    sib_z(3), sib_z(5), sib_z(4), sib_y(2)
    own_z(3)
    along(0, 3, 0, 1)
    own_z(5)
    along(0, 5, 1, 7)
    own_z(4)
    along(1, 4, 0, 2, lower)
    along(1, 4, 1, 6, upper)
    sib_y(1), sib_y(3)
    own_y(2)
    sib_z(1), sib_z(7)
    own_y(1), own_y(3)
    sib_z(2), sib_z(6)
    own_z(1)
    along(2, 1, 0, 1)
    own_z(7)
    along(2, 7, 1, 7)
    sib_y(0), sib_z(0)
    every = tuple(range(NY))
    wait_z(0, 0), wait_z(1, 0, lower)
    own_z(2, ((0, every), (1, (0, 1))))
    along(3, 2, 0, 2)
    wait_z(0, 1), wait_z(1, 1, upper)
    own_z(6, ((4, every), (5, (2, 3))))
    along(3, 6, 1, 6)

    has_y(0)
    for d in (1, 3, 2):
        arrived(ry.at[d], ys.at[d], yr.at[d], off_y(d))
    for d in (4, 3, 5, 2, 6, 1, 7, 0):
        k = (z + d) % NZ
        v = sum_y(0, k) + (ry[1, k].astype(F32) + ry[2, k].astype(F32)) + ry[3, k].astype(F32)
        if d:
            o2[d] = v.astype(BF16)
            send(o2.at[d], r2.at[d], s2.at[d], q2.at[d], off_z(d))
        else:
            keep[1] = v
    has_z(0)
    for way in range(2):
        wait_z(2, way), wait_z(3, way)
    for d in (2, 1, 3, 0):
        k = (y + d) % NY
        v = sum_z(0, k) + (rz[2, k].astype(F32) + rz[3, k].astype(F32)) + (rz[6, k].astype(F32) + rz[7, k].astype(F32))
        if d:
            o3[d] = v.astype(BF16)
            send(o3.at[d], r3.at[d], s3.at[d], q3.at[d], off_y(d))
        else:
            keep[0] = v
    load_ur.wait()
    load_ui.wait()

    def blk(j, zz, yy, n=1):
        return g.at[pl.ds((c * 2 + j) * (UPPER // 4) + ((zz + NZ) % NZ) * NY + (yy + NY) % NY, n)]

    def solve(j, total):
        v = (ur[j] - total).astype(BF16)
        h = lax.dot_general(v, ui[j], NT, preferred_element_type=F32).astype(BF16)
        s = lax.dot_general(h, ui[j], NN, preferred_element_type=F32)
        us[j] = s
        g[(c * 2 + j) * (UPPER // 4) + z * NY + y] = s.astype(BF16)

    def out1(d):
        b = blk(1, z - d, y)
        for dy in (2, 1, 3):
            send(b, b, ays.at[dy, d], ayr.at[dy, d], off_y(dy))
        send(b, b, b1s.at[0, d], b1r.at[0, d], sibling)

    n_sums = len(sends)
    total = keep[1]
    for d in (1, 7, 2, 6, 3, 5, 4):
        arrived(r2.at[d], s2.at[d], q2.at[d], off_z(d))
        total = total + r2[d].astype(F32)
    solve(1, total)
    b = blk(1, z, y)
    for d in (4, 3, 5, 2, 6, 1, 7):
        send(b, b, azs.at[d], azr.at[d], off_z(d))
    out1(0)

    total = keep[0]
    for d in (1, 3, 2):
        arrived(r3.at[d], s3.at[d], q3.at[d], off_y(d))
        total = total + r3[d].astype(F32)
    solve(0, total)
    b = blk(0, z, y)
    for d in (2, 1, 3):
        send(b, b, aws.at[d], awr.at[d], off_y(d))
    for cp in sends[:n_sums]:
        cp.wait_send()

    def in1(d):
        b = blk(1, z - d, y)
        arrived(b, azs.at[d], azr.at[d], off_z(d))
        out1(d)

    def along_y(d):
        for dy in (1, 3, 2):
            b = blk(1, z - d, y - dy)
            arrived(b, ays.at[dy, d], ayr.at[dy, d], off_y(dy))
            send(b, b, b1s.at[dy, d], b1r.at[dy, d], sibling)

    def ring_piece(way, k, mine=0):
        s, first = ((1, 0), (2, 1), (2, 0), (3, 1), (3, 0), (4, 1))[k]
        s = s - mine
        zz = z - s if way == 0 else z + s
        return (zz, 0, NY) if k == 0 else (zz, 2 * (1 - first if way == 0 else first), 2)

    def hop(way, n):
        return off_z(n if way == 0 else NZ - n)

    def along_z(k):
        for way in range(2):
            b = blk(0, *ring_piece(way, k))
            arrived(b, ars.at[way, k], arr.at[way, k], hop(way, 1))
            if k in (1, 2):
                send(b, b, ars.at[way, k + 2], arr.at[way, k + 2], hop(way, 1))
            if k == 1:
                send(b, b, ars.at[way, 5], arr.at[way, 5], hop(way, 2))
            send(b, b, b0s.at[way, k], b0r.at[way, k], sibling)

    in1(1), in1(7)
    for d in (1, 3, 2):
        b = blk(0, z, y - d)
        arrived(b, aws.at[d], awr.at[d], off_y(d))
    for k in (1, 2, 0):
        for way in range(2):
            b = blk(0, *ring_piece(way, k, 2 if k else 1))
            send(b, b, ars.at[way, k], arr.at[way, k], hop(way, 2 if k else 1))
    b = blk(0, z, 0, NY)
    send(b, b, b0s.at[0, 6], b0r.at[0, 6], sibling)
    in1(2), in1(6), along_y(0), in1(3), in1(5), in1(4)
    along_y(1), along_y(7), along_y(2), along_y(6), along_z(1), along_z(2)
    along_y(3), along_y(5), along_z(0), along_y(4), along_z(3), along_z(4), along_z(5)

    def there(j, zz, yy, n=1):
        return g.at[pl.ds(((1 - c) * 2 + j) * (UPPER // 4) + ((zz + NZ) % NZ) * NY + (yy + NY) % NY, n)]

    for d in range(NZ):
        for dy in range(NY):
            arrived(there(1, z - d, y - dy), b1s.at[dy, d], b1r.at[dy, d], sibling)
    arrived(there(0, z, 0, NY), b0s.at[0, 6], b0r.at[0, 6], sibling)
    for k in range(6):
        for way in range(2):
            arrived(there(0, *ring_piece(way, k)), b0s.at[way, k], b0r.at[way, k], sibling)

    def backward(i, _):
        backs = []
        for q in range(8):
            n = i * 8 + q
            parts = []
            for b in range(PER):
                k = n * PER + b
                parts.append(g[idx_s[CAP + k // W, k % W]])
            corr = lax.dot_general(
                jnp.concatenate(parts, axis=1), u[pl.ds(n * PER, PER)].reshape(PER * W, W), NN, preferred_element_type=F32
            )
            backs.append((lf[n] - corr).astype(BF16))
        for q in range(8):
            lo[i * 8 + q] = lax.dot_general(backs[q], inv[i, q], NN, preferred_element_type=F32)
        return 0

    lax.fori_loop(0, 4, backward, 0)
    for cp in sends[n_sums:]:
        cp.wait_send()


def on_device(leaf_right, upper_right, leaf_inverse, upper_inverse, update_blocks, block_target, upper_place):
    hbm = pl.BlockSpec(memory_space=pltpu.HBM)
    vmem = pl.BlockSpec(memory_space=pltpu.VMEM)
    dma = pltpu.SemaphoreType.DMA
    leaves = NX * GROUP
    half = lambda *shape: pltpu.VMEM(shape + (COLS, W), BF16)
    wide = lambda *shape: pltpu.VMEM(shape + (COLS, W), F32)
    return pl.pallas_call(
        kernel,
        out_shape=(pltpu.VMEM((leaves, COLS, W), F32), pltpu.VMEM((2, COLS, W), F32)),
        in_specs=[vmem, vmem] + [hbm] * 5,
        out_specs=(vmem, vmem),
        scratch_shapes=[
            pltpu.VMEM((BLOCKS, W, W), BF16),
            wide(leaves),
            pltpu.VMEM((NX, 2, 2, 9, STRIP, W), BF16),
            pltpu.VMEM((NX, GROUP, W, W), BF16),
            wide(leaves),
            wide(BLOCKS + 1),
            pltpu.VMEM((8, W), I32),
            pltpu.SMEM((8, W), I32),
            half(NZ, NY), half(NY, NZ),
            half(NZ, NY), half(NY, NZ),
            half(NZ, NY), half(NY, NZ),
            half(8, NY), half(NY, NZ),
            half(NZ), half(NZ),
            half(NY), half(NY),
            wide(2),
            wide(2),
            pltpu.VMEM((2, W, W), BF16),
            half(UPPER),
            dma((32,)),
            dma((8, 2)), dma((8, 2)),
            dma((NZ,)), dma((NZ,)), dma((NY,)), dma((NY,)),
            dma((2, 4)), dma((2, 4)), dma((NY,)), dma((NY,)),
            dma((NZ,)), dma((NZ,)), dma((NY,)), dma((NY,)),
            dma((NZ,)), dma((NZ,)),
            dma((NY, NZ)), dma((NY, NZ)),
            dma((NY,)), dma((NY,)),
            dma((2, 6)), dma((2, 6)),
            dma((4, NZ)), dma((4, NZ)),
            dma((2, 7)), dma((2, 7)),
            pltpu.SemaphoreType.REGULAR((4,)),
        ],
        compiler_params=pltpu.CompilerParams(
            collective_id=0, has_side_effects=True, vmem_limit_bytes=59 * 2**20
        ),
        name="solve",
    )(block_target.reshape(1, -1), upper_place.reshape(1, -1), leaf_right, upper_right, leaf_inverse, upper_inverse, update_blocks)


def solution(mesh):
    return jax.shard_map(
        on_device,
        mesh=mesh,
        in_specs=(
            P("leaf", "rhs", None),
            P("leaf", "rhs", None),
            P(("leaf", "rhs"), None, None),
            P("leaf", None, None),
            P("leaf", None, None),
            P("leaf", None),
            P(),
        ),
        out_specs=(P("leaf", "rhs", None), P("leaf", "rhs", None)),
        check_vma=False,
    )
```

time: 72.1 us -> 60.1 us (0.83)
  Pallas kernels: 67.5 us -> 57.8 us
  local copies, waits for them, and re-layouts: 3.78 us -> 1.6 us
    pallas_call x1, Pallas kernels: 67.5 us -> 57.8 us  [on_device(): pl.pallas_call(kernel, out_shape=(pltpu.VMEM((leaves, COLS, W), F32), plt...]
    unnamed x2, local copies, waits for them, and re-layouts: 3.78 us -> 1.6 us
where the time goes in v3:
time: 60.1 us; the launch traced here: 60 us
  Pallas kernels  57.8 us (96%)
  local copies, waits for them, and re-layouts  1.6 us (3%)
  between operations  0.64 us (1%)
    pallas_call x1, Pallas kernels, on_device(): pl.pallas_call(kernel, out_shape=(pltpu.VMEM((leaves, COLS, W), F32), plt...  57.8 us
    unnamed x2, local copies, waits for them, and re-layouts  1.6 us

profile of v3, /device:TPU:1, one launch (start us, length us, event | category | flops | bytes accessed | tf_op | source)
XLA Modules:
  0.0 60.0 jit_solution(1934009638282676718)
XLA Ops:
  0.6 57.8 %solve.1 = (f32[32,64,128]{2,1,0:T(8,128)S(1)}, f32[2,64,128]{2,1,0:T(8,128)S(1)}) custom-call(s32[1,256]{1,0:T(1,128)} %bitcast.2, s32[1,128]{1,0:T(1,128)} %bitcast.3, f32[32,64,128]{2,1,0:T(8,128)} %right_hbm.1, f32[2,64,128]{2,1,0:T(8,128)} %upper_right_hbm.1, bf16[8,128,128]{2,1,0:T(8,128)(2,1)} %inv_hbm.1, bf16[2,128,128]{2,1,0:T(8,128)(2,1)} %upper_inv_hbm.1, ...), custom_call_target="tpu_custom_call" | custom-call | tf_op jit(solution)/shard_map/solve/pallas_call | solution.py:450
  58.4 1.0 %copy.11 = f32[32,64,128]{2,1,0:T(8,128)} copy(f32[32,64,128]{2,1,0:T(8,128)S(1)} %get-tuple-element.2) | data formatting | bytes 2097152
  59.4 0.6 %copy.12 = f32[2,64,128]{2,1,0:T(8,128)} copy(f32[2,64,128]{2,1,0:T(8,128)S(1)} %get-tuple-element.3) | data formatting | bytes 131072

commit v4 on v3

v4 whole, which is shorter than its diff:
```python
import jax
import jax.numpy as jnp
from jax import lax
from jax.experimental import pallas as pl
from jax.experimental.pallas import tpu as pltpu
from jax.sharding import PartitionSpec as P

MESH = pl.DeviceIdType.MESH
F32, BF16, I32 = jnp.float32, jnp.bfloat16, jnp.int32
NX, NY, NZ, NC = 4, 4, 8, 2
PER = 8
GROUP = 8
COLS, W = 64, 128
BLOCKS = 256
CAP = 4
UPPER = NY * NZ * NC * 2
STRIP = 16
NT = (((1,), (1,)), ((), ()))
NN = (((1,), (0,)), ((), ()))


def kernel(
    target_hbm, place_hbm, right_hbm, upper_right_hbm, inv_hbm, upper_inv_hbm, u_hbm,
    lo, us,
    target_ref, place_ref, u, x, pk, inv, lf, t, idx_v, idx_s, az, ay, bz, by, oz, oy, rz, ry,
    o2, r2, o3, r3, keep, ur, ui, g,
    loc, xr, crz, cry, zr, last_z, yr, q2, q3, azr, ayr, awr, arr, br,
    xs, csz, csy, zs, ys, s2, s3, gs, ready,
):
    leaf, rx = lax.axis_index("leaf"), lax.axis_index("rhs")
    y, z, c = leaf // (NZ * NC), (leaf // NC) % NZ, leaf % NC

    def at(yy, zz, cc, xx):
        return ((yy * NZ + zz) * NC + cc, xx)

    def off_x(d):
        return at(y, z, c, (rx + d) % NX)

    def off_y(d):
        return at((y + d) % NY, z, c, rx)

    def off_z(d):
        return at(y, (z + d) % NZ, c, rx)

    sibling = at(y, z, 1 - c, rx)

    def remote(src, dst, ssem, rsem, dev):
        return pltpu.make_async_remote_copy(
            src_ref=src, dst_ref=dst, send_sem=ssem, recv_sem=rsem, device_id=dev, device_id_type=MESH
        )

    def send(src, dst, ssem, rsem, dev):
        remote(src, dst, ssem, rsem, dev).start()

    def arrived(ref, rsem):
        remote(ref, ref, xs, rsem, sibling).wait_recv()

    def sent(ref, ssem):
        remote(ref, ref, ssem, br, sibling).wait_send()

    barrier = pltpu.get_barrier_semaphore()
    peers = [off_x(1), off_x(3)] + [off_y(1), off_y(3), off_z(1), off_z(7), sibling]
    for dev in peers:
        pl.semaphore_signal(barrier, inc=1, device_id=dev, device_id_type=MESH)

    own = pltpu.make_async_copy(inv_hbm, inv.at[rx], loc.at[0])
    own.start()
    load_target = pltpu.make_async_copy(target_hbm, target_ref, loc.at[5])
    load_target.start()
    load_place = pltpu.make_async_copy(place_hbm, place_ref, loc.at[6])
    load_place.start()

    def pair_of(i, m):
        d = jnp.where(i < 2, 0, jnp.where(i >= 6, 2, 1 + 2 * (i % 2)))
        half = jnp.where(i >= 6, m, jnp.where((i == 4) | (i == 5), 1 - i % 2, i % 2))
        return (rx + NX - d) % NX, half, jnp.where(i >= 6, i % 2, m)

    def load_u(i, m):
        src, half, q = pair_of(i, m)
        part = pl.ds((src * 4 + half * 2 + q) * (2 * PER), 2 * PER)
        return pltpu.make_async_copy(u_hbm.at[part], u.at[part], loc.at[7 + i])

    load_x = pltpu.make_async_copy(right_hbm, x, loc.at[1])
    load_x.start()

    def start_u(i, _):
        load_u(i, 0).start()
        load_u(i, 1).start()
        return 0

    lax.fori_loop(0, 8, start_u, 0)
    load_ur = pltpu.make_async_copy(upper_right_hbm, ur, loc.at[2])
    load_ur.start()
    load_ui = pltpu.make_async_copy(upper_inv_hbm, ui, loc.at[3])
    load_ui.start()

    own.wait()
    lane16 = lax.broadcasted_iota(I32, (STRIP, W), 1)

    def strip(n, s):
        return inv[rx, n, s * STRIP : (s + 1) * STRIP, :].astype(F32)

    for h in range(2):
        for q in range(2):
            two = (h * 4 + q * 2, h * 4 + q * 2 + 1)
            for m, n in enumerate(two):
                for s in range(3):
                    pk[rx, h, q, m * 3 + s] = (strip(n, 6 - s) + pltpu.roll(strip(n, s), STRIP * (7 - s), 1)).astype(BF16)
                pk[rx, h, q, 6 + m] = inv[rx, n, 7 * STRIP :, :]
            pk[rx, h, q, 8] = (strip(two[0], 3) + pltpu.roll(strip(two[1], 3), W // 2, 1)).astype(BF16)

    pl.semaphore_wait(barrier, len(peers))

    def pass_on(i, near):
        for d in (near, NZ - near):
            pl.semaphore_signal(ready.at[i], inc=1, device_id=off_z(d), device_id_type=MESH)

    pass_on(0, 1)
    for d in (1, NY - 1):
        pl.semaphore_signal(ready.at[2], inc=1, device_id=off_y(d), device_id_type=MESH)

    for h, i, d in ((0, 2, 1), (1, 3, 3), (1, 4, 1), (0, 5, 3)):
        for q in range(2):
            b = pk.at[rx, h, q]
            send(b, b, xs, xr.at[i - 2, q], off_x(d))
    relays = []
    for h, d in ((0, 1), (1, 3)):
        for q in range(2):
            b = pk.at[(rx + NX - d) % NX, h, q]
            relays.append(remote(b, b, xs, xr.at[4 + q, h], off_x(d)))
    load_target.wait()
    load_place.wait()
    lane = lax.broadcasted_iota(I32, (BLOCKS, W), 1)
    row = lax.broadcasted_iota(I32, (BLOCKS, W), 0)
    target = jnp.concatenate(
        [
            jnp.sum(jnp.where(lane[:W] == row[:W], target_ref[:, h * W : (h + 1) * W], 0), axis=1, keepdims=True)
            for h in range(BLOCKS // W)
        ],
        axis=0,
    )
    pos = jnp.sum(jnp.where(target == lane, place_ref[...], 0), axis=1, keepdims=True)
    cand = jnp.where(pos == lane, row, BLOCKS)
    for s in range(CAP):
        low = jnp.min(cand, axis=0, keepdims=True)
        idx_v[s : s + 1, :] = low
        cand = jnp.where(cand > low, cand, BLOCKS)
    where_in_g = (((pos // 2) % 2) * 2 + pos % 2) * (UPPER // 4) + ((pos // 4) % NZ) * NY + pos // (4 * NZ)
    for h in range(BLOCKS // W):
        idx_v[CAP + h : CAP + h + 1, :] = jnp.sum(jnp.where(row - h * W == lane, where_in_g, 0), axis=0, keepdims=True)
    idx_v[CAP + 2 :, :] = jnp.zeros((8 - CAP - 2, W), I32)
    to_smem = pltpu.make_async_copy(idx_v, idx_s, loc.at[4])
    to_smem.start()

    t[BLOCKS] = jnp.zeros((COLS, W), F32)
    load_x.wait()

    def forward(i, _):
        @pl.when(i == 2)
        def _():
            pl.semaphore_wait(ready.at[0], 2)
            pass_on(1, 2)

        @pl.when(i >= 2)
        def _():
            for m in range(2):
                src, half, q = pair_of(i, m)
                arrived(pk.at[src, half, q], xr.at[i - 2, m])
                for h in range(2):

                    @pl.when(i == 2 + h)
                    def _():
                        relays[2 * h + m].start()

            for m in range(2):
                src, half, q = pair_of(i, m)
                for e in range(2):
                    n = half * 4 + q * 2 + e
                    for s in range(3):
                        both = pk[src, half, q, e * 3 + s].astype(F32)
                        cut = STRIP * (7 - s)
                        inv[src, n, (6 - s) * STRIP : (7 - s) * STRIP, :] = jnp.where(lane16 < cut, both, 0.0).astype(BF16)
                        inv[src, n, s * STRIP : (s + 1) * STRIP, :] = jnp.where(
                            lane16 < W - cut, pltpu.roll(both, W - cut, 1), 0.0
                        ).astype(BF16)
                    inv[src, n, 7 * STRIP :, :] = pk[src, half, q, 6 + e]
                    both = pk[src, half, q, 8].astype(F32)
                    if e:
                        both = pltpu.roll(both, W // 2, 1)
                    inv[src, n, 3 * STRIP : 4 * STRIP, :] = jnp.where(lane16 < W // 2, both, 0.0).astype(BF16)

        some = u.at[pl.ds(0, 4 * PER)]
        pltpu.make_async_copy(some, some, loc.at[7 + i]).wait()
        solved = []
        for m in range(2):
            src, half, q = pair_of(i, m)
            for e in range(2):
                within = half * 4 + q * 2 + e
                n = src * GROUP + within
                f = lax.dot_general(x[n].astype(BF16), inv[src, within], NT, preferred_element_type=F32)
                lf[n] = f
                solved.append((n, f.astype(BF16)))
        for n, f in solved:
            r = lax.dot_general(f, u[pl.ds(n * PER, PER)].reshape(PER * W, W), NT, preferred_element_type=F32)
            for b in range(PER):
                t[n * PER + b] = r[:, b * W : (b + 1) * W]
        return 0

    lax.fori_loop(0, 8, forward, 0)
    to_smem.wait()
    pl.semaphore_wait(ready.at[1], 2)
    pl.semaphore_wait(ready.at[2], 2)

    def sum_of(p):
        return (t[idx_s[0, p]] + t[idx_s[1, p]]) + (t[idx_s[2, p]] + t[idx_s[3, p]])

    def at_z(d, yy, cc):
        return ((yy * NZ + (z + d) % NZ) * NC + cc) * 2

    z_order = (4, 3, 5, 2, 6, 1, 7, 0)

    def at_y(d, k, cc):
        return ((((y + d) % NY) * NZ + (z + z_order[k]) % NZ) * NC + cc) * 2 + 1

    def sib_z(d):
        sums = [sum_of(at_z(d, k, 1 - c)).astype(BF16) for k in range(NY)]
        for k in range(NY):
            az[d, k] = sums[k]
        send(az.at[d], bz.at[d], csz, crz.at[d], sibling)

    def sib_y(d):
        for h in range(0, NZ, 4):
            sums = [sum_of(at_y(d, h + k, 1 - c)).astype(BF16) for k in range(4)]
            for k in range(4):
                ay[d, h + k] = sums[k]
        send(ay.at[d], by.at[d], csy, cry.at[d], sibling)

    def has_z(d):
        arrived(bz.at[d], crz.at[d])

    def has_y(d):
        arrived(by.at[d], cry.at[d])

    def sum_z(d, k):
        return sum_of(at_z(d, k, c)) + bz[d, k].astype(F32)

    def sum_y(d, k):
        return sum_of(at_y(d, k, c)) + by[d, k].astype(F32)

    lower, upper = pl.ds(0, 2), pl.ds(2, 2)

    def own_z(d, part, more=()):
        sums = []
        for k in part:
            v = sum_z(d, k)
            for got in more:
                v = v + rz[got, k].astype(F32)
            sums.append(v.astype(BF16))
        for k, v in zip(part, sums):
            oz[d, k] = v

    def along(kind, d, way, to, part, sem):
        here = pl.ds(part[0], len(part))
        send(oz.at[d, here], rz.at[way * 4 + kind, here], zs, sem, off_z(to if way == 0 else NZ - to))

    def wait_z(kind, way, part, sem):
        arrived(rz.at[way * 4 + kind, pl.ds(part[0], len(part))], sem)

    def own_y(d, h):
        sums = [sum_y(d, h + k).astype(BF16) for k in range(4)]
        for k in range(4):
            oy[d, h + k] = sums[k]
        here = pl.ds(h, 4)
        send(oy.at[d, here], ry.at[d, here], ys, yr.at[h // 4], off_y(d))

    lower, upper, every = (0, 1), (2, 3), (0, 1, 2, 3)
    firsts, seconds = (lower, upper), (upper, lower)
    sib_z(4), sib_z(3), sib_z(5), sib_y(2)
    has_z(4)
    own_z(4, every)
    for way in range(2):
        along(1, 4, way, 2, firsts[way], zr.at[way, 0])
    for way, d in ((0, 3), (1, 5)):
        has_z(d)
        own_z(d, every)
        along(0, d, way, 1, firsts[way], zr.at[way, 1])
    for way, d in ((0, 3), (1, 5)):
        along(0, d, way, 1, seconds[way], zr.at[way, 2])
    sib_y(1), sib_y(3), sib_z(1), sib_z(7)
    has_y(2)
    own_y(2, 0)
    has_y(1)
    own_y(1, 0)
    has_y(3)
    own_y(3, 0)
    for d in (2, 1, 3):
        own_y(d, 4)
    for way, d in ((0, 1), (1, 7)):
        has_z(d)
        own_z(d, every)
        along(2, d, way, 1, every, last_z)
    sib_z(2), sib_z(6), sib_y(0), sib_z(0)
    for way, d in ((0, 2), (1, 6)):
        has_z(d)
        wait_z(1, way, firsts[way], zr.at[way, 0])
        wait_z(0, way, firsts[way], zr.at[way, 1])
        own_z(d, firsts[way], (way * 4, way * 4 + 1))
        along(3, d, way, 2, firsts[way], last_z)
    for way, d in ((0, 2), (1, 6)):
        wait_z(0, way, seconds[way], zr.at[way, 2])
        own_z(d, seconds[way], (way * 4,))
        along(3, d, way, 2, seconds[way], last_z)

    has_y(0)
    for h in range(2):
        arrived(ry.at[pl.ds(1, 3), pl.ds(4 * h, 4)], yr.at[h])
        for k in range(4 * h, 4 * h + 4):
            d = z_order[k]
            v = sum_y(0, k) + (ry[1, k].astype(F32) + ry[2, k].astype(F32)) + ry[3, k].astype(F32)
            if d:
                o2[d] = v.astype(BF16)
                send(o2.at[d], r2.at[d], s2, q2, off_z(d))
            else:
                keep[1] = v
    has_z(0)
    arrived(rz.at[pl.ds(0, 4)], last_z)
    for d in (2, 1, 3, 0):
        k = (y + d) % NY
        v = sum_z(0, k) + (rz[2, k].astype(F32) + rz[3, k].astype(F32)) + (rz[6, k].astype(F32) + rz[7, k].astype(F32))
        if d:
            o3[d] = v.astype(BF16)
            send(o3.at[d], r3.at[d], s3, q3, off_y(d))
        else:
            keep[0] = v
    load_ur.wait()
    load_ui.wait()

    def blk(j, zz, yy, n=1):
        return g.at[pl.ds((c * 2 + j) * (UPPER // 4) + ((zz + NZ) % NZ) * NY + (yy + NY) % NY, n)]

    def solve(j, total):
        v = (ur[j] - total).astype(BF16)
        h = lax.dot_general(v, ui[j], NT, preferred_element_type=F32).astype(BF16)
        s = lax.dot_general(h, ui[j], NN, preferred_element_type=F32)
        us[j] = s
        g[(c * 2 + j) * (UPPER // 4) + z * NY + y] = s.astype(BF16)

    def out1(d):
        b = blk(1, z - d, y)
        for dy in (2, 1, 3):
            send(b, b, gs, ayr.at[d], off_y(dy))
        send(b, b, gs, br, sibling)

    total = keep[1]
    arrived(r2.at[pl.ds(1, NZ - 1)], q2)
    for d in range(1, NZ):
        total = total + r2[d].astype(F32)
    solve(1, total)
    b = blk(1, z, y)
    for d in (4, 3, 5, 2, 6, 1, 7):
        send(b, b, gs, azr.at[d], off_z(d))
    out1(0)

    total = keep[0]
    arrived(r3.at[pl.ds(1, NY - 1)], q3)
    for d in range(1, NY):
        total = total + r3[d].astype(F32)
    solve(0, total)
    b = blk(0, z, y)
    for d in (2, 1, 3):
        send(b, b, gs, awr, off_y(d))

    def in1(d):
        arrived(blk(1, z - d, y), azr.at[d])
        out1(d)

    def along_y(d):
        arrived(g.at[pl.ds(0, NY - 1)], ayr.at[d])
        for dy in (1, 3, 2):
            b = blk(1, z - d, y - dy)
            send(b, b, gs, br, sibling)

    def ring_piece(way, k, mine=0):
        s, first = ((1, 0), (2, 1), (2, 0), (3, 1), (3, 0), (4, 1))[k]
        s = s - mine
        zz = z - s if way == 0 else z + s
        return (zz, 0, NY) if k == 0 else (zz, 2 * (1 - first if way == 0 else first), 2)

    def hop(way, n):
        return off_z(n if way == 0 else NZ - n)

    def along_z(k):
        for way in range(2):
            b = blk(0, *ring_piece(way, k))
            arrived(b, arr.at[way, k])
            if k in (1, 2):
                send(b, b, gs, arr.at[way, k + 2], hop(way, 1))
            if k == 1:
                send(b, b, gs, arr.at[way, 5], hop(way, 2))
            send(b, b, gs, br, sibling)

    in1(1), in1(7)
    arrived(g.at[pl.ds(0, NY - 1)], awr)
    for k in (1, 2, 0):
        for way in range(2):
            b = blk(0, *ring_piece(way, k, 2 if k else 1))
            send(b, b, gs, arr.at[way, k], hop(way, 2 if k else 1))
    b = blk(0, z, 0, NY)
    send(b, b, gs, br, sibling)
    in1(2), in1(6), along_y(0), in1(3), in1(5), in1(4)
    along_y(1), along_y(7), along_y(2), along_y(6), along_z(1), along_z(2)
    along_y(3), along_y(5), along_z(0), along_y(4), along_z(3), along_z(4), along_z(5)
    arrived(g.at[pl.ds(0, UPPER // 2)], br)

    def backward(i, _):
        backs = []
        for q in range(8):
            n = i * 8 + q
            parts = []
            for b in range(PER):
                k = n * PER + b
                parts.append(g[idx_s[CAP + k // W, k % W]])
            corr = lax.dot_general(
                jnp.concatenate(parts, axis=1), u[pl.ds(n * PER, PER)].reshape(PER * W, W), NN, preferred_element_type=F32
            )
            backs.append((lf[n] - corr).astype(BF16))
        for q in range(8):
            lo[i * 8 + q] = lax.dot_general(backs[q], inv[i, q], NN, preferred_element_type=F32)
        return 0

    lax.fori_loop(0, 4, backward, 0)
    sent(pk.at[pl.ds(0, 3)], xs)
    sent(az, csz)
    sent(ay, csy)
    sent(oz.at[pl.ds(0, 7)], zs)
    sent(oy.at[pl.ds(0, 3)], ys)
    sent(o2.at[pl.ds(0, NZ - 1)], s2)
    sent(o3.at[pl.ds(0, NY - 1)], s3)
    sent(g.at[pl.ds(0, 126)], gs)


def on_device(leaf_right, upper_right, leaf_inverse, upper_inverse, update_blocks, block_target, upper_place):
    hbm = pl.BlockSpec(memory_space=pltpu.HBM)
    vmem = pl.BlockSpec(memory_space=pltpu.VMEM)
    dma = pltpu.SemaphoreType.DMA
    leaves = NX * GROUP
    half = lambda *shape: pltpu.VMEM(shape + (COLS, W), BF16)
    wide = lambda *shape: pltpu.VMEM(shape + (COLS, W), F32)
    return pl.pallas_call(
        kernel,
        out_shape=(pltpu.VMEM((leaves, COLS, W), F32), pltpu.VMEM((2, COLS, W), F32)),
        in_specs=[hbm] * 7,
        out_specs=(vmem, vmem),
        scratch_shapes=[
            pltpu.VMEM((1, BLOCKS), I32),
            pltpu.VMEM((1, W), I32),
            pltpu.VMEM((BLOCKS, W, W), BF16),
            wide(leaves),
            pltpu.VMEM((NX, 2, 2, 9, STRIP, W), BF16),
            pltpu.VMEM((NX, GROUP, W, W), BF16),
            wide(leaves),
            wide(BLOCKS + 1),
            pltpu.VMEM((8, W), I32),
            pltpu.SMEM((8, W), I32),
            half(NZ, NY), half(NY, NZ),
            half(NZ, NY), half(NY, NZ),
            half(NZ, NY), half(NY, NZ),
            half(8, NY), half(NY, NZ),
            half(NZ), half(NZ),
            half(NY), half(NY),
            wide(2),
            wide(2),
            pltpu.VMEM((2, W, W), BF16),
            half(UPPER),
            dma((15,)),
            dma((6, 2)),
            dma((NZ,)), dma((NY,)),
            dma((2, 3)), dma, dma((2,)),
            dma, dma,
            dma((NZ,)), dma((NZ,)), dma, dma((2, 6)), dma,
            dma, dma, dma, dma, dma, dma, dma, dma,
            pltpu.SemaphoreType.REGULAR((3,)),
        ],
        compiler_params=pltpu.CompilerParams(
            collective_id=0, has_side_effects=True, vmem_limit_bytes=59 * 2**20
        ),
        name="solve",
    )(block_target.reshape(1, -1), upper_place.reshape(1, -1), leaf_right, upper_right, leaf_inverse, upper_inverse, update_blocks)


def solution(mesh):
    return jax.shard_map(
        on_device,
        mesh=mesh,
        in_specs=(
            P("leaf", "rhs", None),
            P("leaf", "rhs", None),
            P(("leaf", "rhs"), None, None),
            P("leaf", None, None),
            P("leaf", None, None),
            P("leaf", None),
            P(),
        ),
        out_specs=(P("leaf", "rhs", None), P("leaf", "rhs", None)),
        check_vma=False,
    )
```

time: 60.1 us -> 55.3 us (0.920)
  Pallas kernels: 57.8 us -> 53 us
    pallas_call x1, Pallas kernels: 57.8 us -> 53 us  [on_device(): pl.pallas_call(kernel, out_shape=(pltpu.VMEM((leaves, COLS, W), F32), plt...]
where the time goes in v4:
time: 55.3 us; the launch traced here: 55.2 us
  Pallas kernels  53 us (96%)
  local copies, waits for them, and re-layouts  1.6 us (3%)
  between operations  0.64 us (1%)
    pallas_call x1, Pallas kernels, on_device(): pl.pallas_call(kernel, out_shape=(pltpu.VMEM((leaves, COLS, W), F32), plt...  53 us
    unnamed x2, local copies, waits for them, and re-layouts  1.6 us

profile of v4, /device:TPU:1, one launch (start us, length us, event | category | flops | bytes accessed | tf_op | source)
XLA Modules:
  0.0 55.2 jit_solution(12575381112813392517)
XLA Ops:
  0.6 53.0 %solve.1 = (f32[32,64,128]{2,1,0:T(8,128)S(1)}, f32[2,64,128]{2,1,0:T(8,128)S(1)}) custom-call(s32[1,256]{1,0:T(1,128)} %bitcast.2, s32[1,128]{1,0:T(1,128)} %bitcast.3, f32[32,64,128]{2,1,0:T(8,128)} %right_hbm.1, f32[2,64,128]{2,1,0:T(8,128)} %upper_right_hbm.1, bf16[8,128,128]{2,1,0:T(8,128)(2,1)} %inv_hbm.1, bf16[2,128,128]{2,1,0:T(8,128)(2,1)} %upper_inv_hbm.1, ...), custom_call_target="tpu_custom_call" | custom-call | tf_op jit(solution)/shard_map/solve/pallas_call | solution.py:449
  53.6 1.0 %copy.11 = f32[32,64,128]{2,1,0:T(8,128)} copy(f32[32,64,128]{2,1,0:T(8,128)S(1)} %get-tuple-element.2) | data formatting | bytes 2097152
  54.6 0.6 %copy.12 = f32[2,64,128]{2,1,0:T(8,128)} copy(f32[2,64,128]{2,1,0:T(8,128)S(1)} %get-tuple-element.3) | data formatting | bytes 131072

commit v5 on v4

--- a/solution.py
+++ b/solution.py
@@ -23,9 +23,9 @@
     target_hbm, place_hbm, right_hbm, upper_right_hbm, inv_hbm, upper_inv_hbm, u_hbm,
     lo, us,
     target_ref, place_ref, u, x, pk, inv, lf, t, idx_v, idx_s, az, ay, bz, by, oz, oy, rz, ry,
-    o2, r2, o3, r3, keep, ur, ui, g,
-    loc, xr, crz, cry, zr, last_z, yr, q2, q3, azr, ayr, awr, arr, br,
-    xs, csz, csy, zs, ys, s2, s3, gs, ready,
+    o2, r2, r3, keep, ur, ui, ur1, ui1, solved_y, g,
+    loc, xr, crz, cry, zr, last_z, yr, q2, q3, azr, ayr, arr, br, mr,
+    xs, csz, csy, zs, ys, s2, s3, gs, ms, ready,
 ):
     leaf, rx = lax.axis_index("leaf"), lax.axis_index("rhs")
     y, z, c = leaf // (NZ * NC), (leaf // NC) % NZ, leaf % NC
@@ -89,10 +89,14 @@
         return 0
 
     lax.fori_loop(0, 8, start_u, 0)
-    load_ur = pltpu.make_async_copy(upper_right_hbm, ur, loc.at[2])
-    load_ur.start()
-    load_ui = pltpu.make_async_copy(upper_inv_hbm, ui, loc.at[3])
-    load_ui.start()
+    uppers = [
+        pltpu.make_async_copy(upper_right_hbm.at[0], ur.at[y], loc.at[2]),
+        pltpu.make_async_copy(upper_right_hbm.at[1], ur1, loc.at[3]),
+        pltpu.make_async_copy(upper_inv_hbm.at[0], ui.at[y], loc.at[15]),
+        pltpu.make_async_copy(upper_inv_hbm.at[1], ui1, loc.at[16]),
+    ]
+    for cp in uppers:
+        cp.start()
 
     own.wait()
     lane16 = lax.broadcasted_iota(I32, (STRIP, W), 1)
@@ -161,6 +165,15 @@
             pl.semaphore_wait(ready.at[0], 2)
             pass_on(1, 2)
 
+        @pl.when(i == 4)
+        def _():
+            for cp in uppers:
+                cp.wait()
+            pl.semaphore_wait(ready.at[2], 2)
+            for d in (2, 1, 3):
+                send(ui.at[y], ui.at[y], ms.at[0], mr.at[0], off_y(d))
+                send(ur.at[y], ur.at[y], ms.at[1], mr.at[1], off_y(d))
+
         @pl.when(i >= 2)
         def _():
             for m in range(2):
@@ -209,7 +222,6 @@
     lax.fori_loop(0, 8, forward, 0)
     to_smem.wait()
     pl.semaphore_wait(ready.at[1], 2)
-    pl.semaphore_wait(ready.at[2], 2)
 
     def sum_of(p):
         return (t[idx_s[0, p]] + t[idx_s[1, p]]) + (t[idx_s[2, p]] + t[idx_s[3, p]])
@@ -321,29 +333,22 @@
                 o2[d] = v.astype(BF16)
                 send(o2.at[d], r2.at[d], s2, q2, off_z(d))
             else:
-                keep[1] = v
+                keep[...] = v
     has_z(0)
     arrived(rz.at[pl.ds(0, 4)], last_z)
-    for d in (2, 1, 3, 0):
-        k = (y + d) % NY
+    for k in range(NY):
         v = sum_z(0, k) + (rz[2, k].astype(F32) + rz[3, k].astype(F32)) + (rz[6, k].astype(F32) + rz[7, k].astype(F32))
-        if d:
-            o3[d] = v.astype(BF16)
-            send(o3.at[d], r3.at[d], s3, q3, off_y(d))
-        else:
-            keep[0] = v
-    load_ur.wait()
-    load_ui.wait()
+        r3[y, k] = v.astype(BF16)
+    for d in (2, 1, 3):
+        send(r3.at[y], r3.at[y], s3, q3, off_y(d))
 
     def blk(j, zz, yy, n=1):
         return g.at[pl.ds((c * 2 + j) * (UPPER // 4) + ((zz + NZ) % NZ) * NY + (yy + NY) % NY, n)]
 
-    def solve(j, total):
-        v = (ur[j] - total).astype(BF16)
-        h = lax.dot_general(v, ui[j], NT, preferred_element_type=F32).astype(BF16)
-        s = lax.dot_general(h, ui[j], NN, preferred_element_type=F32)
-        us[j] = s
-        g[(c * 2 + j) * (UPPER // 4) + z * NY + y] = s.astype(BF16)
+    def solve(right, total, factor):
+        v = (right - total).astype(BF16)
+        h = lax.dot_general(v, factor, NT, preferred_element_type=F32).astype(BF16)
+        return lax.dot_general(h, factor, NN, preferred_element_type=F32)
 
     def out1(d):
         b = blk(1, z - d, y)
@@ -351,24 +356,27 @@
             send(b, b, gs, ayr.at[d], off_y(dy))
         send(b, b, gs, br, sibling)
 
-    total = keep[1]
+    total = keep[...]
     arrived(r2.at[pl.ds(1, NZ - 1)], q2)
     for d in range(1, NZ):
         total = total + r2[d].astype(F32)
-    solve(1, total)
+    v = solve(ur1[...], total, ui1[...])
+    us[1] = v
+    g[(c * 2 + 1) * (UPPER // 4) + z * NY + y] = v.astype(BF16)
     b = blk(1, z, y)
     for d in (4, 3, 5, 2, 6, 1, 7):
         send(b, b, gs, azr.at[d], off_z(d))
     out1(0)
 
-    total = keep[0]
-    arrived(r3.at[pl.ds(1, NY - 1)], q3)
-    for d in range(1, NY):
-        total = total + r3[d].astype(F32)
-    solve(0, total)
-    b = blk(0, z, y)
-    for d in (2, 1, 3):
-        send(b, b, gs, awr, off_y(d))
+    arrived(ui.at[pl.ds(0, NY - 1)], mr.at[0])
+    arrived(ur.at[pl.ds(0, NY - 1)], mr.at[1])
+    arrived(r3.at[pl.ds(0, NY - 1)], q3)
+    for k in range(NY):
+        total = (r3[0, k].astype(F32) + r3[1, k].astype(F32)) + (r3[2, k].astype(F32) + r3[3, k].astype(F32))
+        v = solve(ur[k], total, ui[k])
+        solved_y[k] = v
+        g[c * 2 * (UPPER // 4) + z * NY + k] = v.astype(BF16)
+    us[0] = solved_y[y]
 
     def in1(d):
         arrived(blk(1, z - d, y), azr.at[d])
@@ -399,16 +407,14 @@
                 send(b, b, gs, arr.at[way, 5], hop(way, 2))
             send(b, b, gs, br, sibling)
 
-    in1(1), in1(7)
-    arrived(g.at[pl.ds(0, NY - 1)], awr)
     for k in (1, 2, 0):
         for way in range(2):
             b = blk(0, *ring_piece(way, k, 2 if k else 1))
             send(b, b, gs, arr.at[way, k], hop(way, 2 if k else 1))
     b = blk(0, z, 0, NY)
     send(b, b, gs, br, sibling)
-    in1(2), in1(6), along_y(0), in1(3), in1(5), in1(4)
-    along_y(1), along_y(7), along_y(2), along_y(6), along_z(1), along_z(2)
+    in1(1), in1(7), in1(2), in1(6), along_y(0), in1(3), in1(5), in1(4)
+    along_y(1), along_y(7), along_z(1), along_z(2), along_y(2), along_y(6)
     along_y(3), along_y(5), along_z(0), along_y(4), along_z(3), along_z(4), along_z(5)
     arrived(g.at[pl.ds(0, UPPER // 2)], br)
 
@@ -435,8 +441,10 @@
     sent(oz.at[pl.ds(0, 7)], zs)
     sent(oy.at[pl.ds(0, 3)], ys)
     sent(o2.at[pl.ds(0, NZ - 1)], s2)
-    sent(o3.at[pl.ds(0, NY - 1)], s3)
-    sent(g.at[pl.ds(0, 126)], gs)
+    sent(r3.at[pl.ds(0, NY - 1)], s3)
+    sent(g.at[pl.ds(0, 123)], gs)
+    sent(ui.at[pl.ds(0, NY - 1)], ms.at[0])
+    sent(ur.at[pl.ds(0, NY - 1)], ms.at[1])
 
 
 def on_device(leaf_right, upper_right, leaf_inverse, upper_inverse, update_blocks, block_target, upper_place):
@@ -467,18 +475,22 @@
             half(NZ, NY), half(NY, NZ),
             half(8, NY), half(NY, NZ),
             half(NZ), half(NZ),
-            half(NY), half(NY),
-            wide(2),
-            wide(2),
-            pltpu.VMEM((2, W, W), BF16),
+            half(NY, NY),
+            wide(),
+            wide(NY),
+            pltpu.VMEM((NY, W, W), BF16),
+            wide(),
+            pltpu.VMEM((W, W), BF16),
+            wide(NY),
             half(UPPER),
-            dma((15,)),
+            dma((17,)),
             dma((6, 2)),
             dma((NZ,)), dma((NY,)),
             dma((2, 3)), dma, dma((2,)),
             dma, dma,
-            dma((NZ,)), dma((NZ,)), dma, dma((2, 6)), dma,
+            dma((NZ,)), dma((NZ,)), dma((2, 6)), dma, dma((2,)),
             dma, dma, dma, dma, dma, dma, dma, dma,
+            dma((2,)),
             pltpu.SemaphoreType.REGULAR((3,)),
         ],
         compiler_params=pltpu.CompilerParams(

time: 55.3 us -> 54.4 us (0.984)
  Pallas kernels: 53 us -> 52.1 us
    pallas_call x1, Pallas kernels: 53 us -> 52.1 us  [on_device(): pl.pallas_call(kernel, out_shape=(pltpu.VMEM((leaves, COLS, W), F32), plt...]
where the time goes in v5:
time: 54.4 us; the launch traced here: 54.3 us
  Pallas kernels  52.1 us (96%)
  local copies, waits for them, and re-layouts  1.6 us (3%)
  between operations  0.64 us (1%)
    pallas_call x1, Pallas kernels, on_device(): pl.pallas_call(kernel, out_shape=(pltpu.VMEM((leaves, COLS, W), F32), plt...  52.1 us
    unnamed x2, local copies, waits for them, and re-layouts  1.6 us

profile of v5, /device:TPU:1, one launch (start us, length us, event | category | flops | bytes accessed | tf_op | source)
XLA Modules:
  0.0 54.3 jit_solution(18071413759223876166)
XLA Ops:
  0.6 52.1 %solve.1 = (f32[32,64,128]{2,1,0:T(8,128)S(1)}, f32[2,64,128]{2,1,0:T(8,128)S(1)}) custom-call(s32[1,256]{1,0:T(1,128)} %bitcast.2, s32[1,128]{1,0:T(1,128)} %bitcast.3, f32[32,64,128]{2,1,0:T(8,128)} %right_hbm.1, f32[2,64,128]{2,1,0:T(8,128)} %upper_right_hbm.1, bf16[8,128,128]{2,1,0:T(8,128)(2,1)} %inv_hbm.1, bf16[2,128,128]{2,1,0:T(8,128)(2,1)} %upper_inv_hbm.1, ...), custom_call_target="tpu_custom_call" | custom-call | tf_op jit(solution)/shard_map/solve/pallas_call | solution.py:457
  52.7 1.0 %copy.11 = f32[32,64,128]{2,1,0:T(8,128)} copy(f32[32,64,128]{2,1,0:T(8,128)S(1)} %get-tuple-element.2) | data formatting | bytes 2097152
  53.7 0.6 %copy.12 = f32[2,64,128]{2,1,0:T(8,128)} copy(f32[2,64,128]{2,1,0:T(8,128)S(1)} %get-tuple-element.3) | data formatting | bytes 131072

commit v6 on v5

--- a/solution.py
+++ b/solution.py
@@ -413,15 +413,15 @@
             send(b, b, gs, arr.at[way, k], hop(way, 2 if k else 1))
     b = blk(0, z, 0, NY)
     send(b, b, gs, br, sibling)
-    in1(1), in1(7), in1(2), in1(6), along_y(0), in1(3), in1(5), in1(4)
-    along_y(1), along_y(7), along_z(1), along_z(2), along_y(2), along_y(6)
-    along_y(3), along_y(5), along_z(0), along_y(4), along_z(3), along_z(4), along_z(5)
+    in1(1), in1(7), in1(2), in1(6), in1(3), in1(5), along_y(0), in1(4)
+    along_z(1), along_y(1), along_y(7), along_z(2), along_y(2), along_y(6)
+    along_z(0), along_y(3), along_y(5), along_z(3), along_z(5), along_y(4), along_z(4)
     arrived(g.at[pl.ds(0, UPPER // 2)], br)
 
     def backward(i, _):
         backs = []
-        for q in range(8):
-            n = i * 8 + q
+        for q in range(16):
+            n = i * 16 + q
             parts = []
             for b in range(PER):
                 k = n * PER + b
@@ -430,11 +430,11 @@
                 jnp.concatenate(parts, axis=1), u[pl.ds(n * PER, PER)].reshape(PER * W, W), NN, preferred_element_type=F32
             )
             backs.append((lf[n] - corr).astype(BF16))
-        for q in range(8):
-            lo[i * 8 + q] = lax.dot_general(backs[q], inv[i, q], NN, preferred_element_type=F32)
+        for q in range(16):
+            lo[i * 16 + q] = lax.dot_general(backs[q], inv[i * 2 + q // 8, q % 8], NN, preferred_element_type=F32)
         return 0
 
-    lax.fori_loop(0, 4, backward, 0)
+    lax.fori_loop(0, 2, backward, 0)
     sent(pk.at[pl.ds(0, 3)], xs)
     sent(az, csz)
     sent(ay, csy)

time: 54.4 us -> 53 us (0.974)
  Pallas kernels: 52.1 us -> 50.7 us
    pallas_call x1, Pallas kernels: 52.1 us -> 50.7 us  [on_device(): pl.pallas_call(kernel, out_shape=(pltpu.VMEM((leaves, COLS, W), F32), plt...]
where the time goes in v6:
time: 53 us; the launch traced here: 52.9 us
  Pallas kernels  50.7 us (96%)
  local copies, waits for them, and re-layouts  1.6 us (3%)
  between operations  0.64 us (1%)
    pallas_call x1, Pallas kernels, on_device(): pl.pallas_call(kernel, out_shape=(pltpu.VMEM((leaves, COLS, W), F32), plt...  50.7 us
    unnamed x2, local copies, waits for them, and re-layouts  1.6 us

profile of v6, /device:TPU:1, one launch (start us, length us, event | category | flops | bytes accessed | tf_op | source)
XLA Modules:
  0.0 52.9 jit_solution(2447671303592463451)
XLA Ops:
  0.6 50.7 %solve.1 = (f32[32,64,128]{2,1,0:T(8,128)S(1)}, f32[2,64,128]{2,1,0:T(8,128)S(1)}) custom-call(s32[1,256]{1,0:T(1,128)} %bitcast.2, s32[1,128]{1,0:T(1,128)} %bitcast.3, f32[32,64,128]{2,1,0:T(8,128)} %right_hbm.1, f32[2,64,128]{2,1,0:T(8,128)} %upper_right_hbm.1, bf16[8,128,128]{2,1,0:T(8,128)(2,1)} %inv_hbm.1, bf16[2,128,128]{2,1,0:T(8,128)(2,1)} %upper_inv_hbm.1, ...), custom_call_target="tpu_custom_call" | custom-call | tf_op jit(solution)/shard_map/solve/pallas_call | solution.py:457
  51.3 1.0 %copy.11 = f32[32,64,128]{2,1,0:T(8,128)} copy(f32[32,64,128]{2,1,0:T(8,128)S(1)} %get-tuple-element.2) | data formatting | bytes 2097152
  52.3 0.6 %copy.12 = f32[2,64,128]{2,1,0:T(8,128)} copy(f32[2,64,128]{2,1,0:T(8,128)S(1)} %get-tuple-element.3) | data formatting | bytes 131072

commit v7 on v6

--- a/solution.py
+++ b/solution.py
@@ -287,7 +287,10 @@
 
     lower, upper, every = (0, 1), (2, 3), (0, 1, 2, 3)
     firsts, seconds = (lower, upper), (upper, lower)
-    sib_z(4), sib_z(3), sib_z(5), sib_y(2)
+    sib_y(2), sib_y(1), sib_y(3), sib_z(4), sib_z(3), sib_z(5)
+    for d in (2, 1, 3):
+        has_y(d)
+        own_y(d, 0)
     has_z(4)
     own_z(4, every)
     for way in range(2):
@@ -298,15 +301,9 @@
         along(0, d, way, 1, firsts[way], zr.at[way, 1])
     for way, d in ((0, 3), (1, 5)):
         along(0, d, way, 1, seconds[way], zr.at[way, 2])
-    sib_y(1), sib_y(3), sib_z(1), sib_z(7)
-    has_y(2)
-    own_y(2, 0)
-    has_y(1)
-    own_y(1, 0)
-    has_y(3)
-    own_y(3, 0)
     for d in (2, 1, 3):
         own_y(d, 4)
+    sib_z(1), sib_z(7)
     for way, d in ((0, 1), (1, 7)):
         has_z(d)
         own_z(d, every)

time: 53 us -> 53 us (level)
  no operation moved by 1% of the time
where the time goes in v7:
time: 53 us; the launch traced here: 52.9 us
  Pallas kernels  50.7 us (96%)
  local copies, waits for them, and re-layouts  1.6 us (3%)
  between operations  0.64 us (1%)
    pallas_call x1, Pallas kernels, on_device(): pl.pallas_call(kernel, out_shape=(pltpu.VMEM((leaves, COLS, W), F32), plt...  50.7 us
    unnamed x2, local copies, waits for them, and re-layouts  1.6 us

profile of v7, /device:TPU:1, one launch (start us, length us, event | category | flops | bytes accessed | tf_op | source)
XLA Modules:
  0.0 52.9 jit_solution(1237164556623391253)
XLA Ops:
  0.6 50.7 %solve.1 = (f32[32,64,128]{2,1,0:T(8,128)S(1)}, f32[2,64,128]{2,1,0:T(8,128)S(1)}) custom-call(s32[1,256]{1,0:T(1,128)} %bitcast.2, s32[1,128]{1,0:T(1,128)} %bitcast.3, f32[32,64,128]{2,1,0:T(8,128)} %right_hbm.1, f32[2,64,128]{2,1,0:T(8,128)} %upper_right_hbm.1, bf16[8,128,128]{2,1,0:T(8,128)(2,1)} %inv_hbm.1, bf16[2,128,128]{2,1,0:T(8,128)(2,1)} %upper_inv_hbm.1, ...), custom_call_target="tpu_custom_call" | custom-call | tf_op jit(solution)/shard_map/solve/pallas_call | solution.py:454
  51.3 1.0 %copy.11 = f32[32,64,128]{2,1,0:T(8,128)} copy(f32[32,64,128]{2,1,0:T(8,128)S(1)} %get-tuple-element.2) | data formatting | bytes 2097152
  52.3 0.6 %copy.12 = f32[2,64,128]{2,1,0:T(8,128)} copy(f32[2,64,128]{2,1,0:T(8,128)S(1)} %get-tuple-element.3) | data formatting | bytes 131072
